TPU v7x, 128 devices: a whole 4x4x4 slice. The times are simulated.
128 devices in a mesh: grp: 4 (over x), smp: 32 (over y, z, core).
Axes of the slice: x: 4, y: 4, z: 4, core: 2. Of those that a mesh axis runs over, the one named last changes fastest.
Arguments:
- currents: bfloat16 [2, 8, 1048576], P(None, None, ('grp', 'smp')), may hold values from -6 to 6
- near_blocks: bfloat16 [2, 32768, 32, 256], P(None, ('grp', 'smp')), may hold values from -0.25 to 0.25
- near_list: int32 [32768, 8], P(('grp', 'smp')), may hold values from 0 to 32767, as said below
- near_count: int32 [32768], P(('grp', 'smp')), may hold values from 1 to 8, as said below
- radiation: bfloat16 [2, 32768, 32, 128], P(None, ('grp', 'smp')), may hold values from -0.75 to 0.75
- interp: bfloat16 [64, 1024], replicated, may hold values from -0.75 to 0.75
- shift_angle: float32 [8, 1024], replicated, may hold values from -3.140625 to 3.140625
- translation: bfloat16 [2, 316, 2048], P(None, None, ('grp', 'smp')), may hold values from -0.0625 to 0.0625
- trans_box: int32 [4096, 12], replicated, may hold values from 0 to 4095
- trans_off: int32 [4096, 12], replicated, may hold values from 0 to 315
Outputs:
- product_field: float32 [2, 8, 1048576], P(None, None, ('grp', 'smp'))
Inputs may be any that keep to these rules, and one draw needn't show every extreme that they name: `near_list`: entry 0 of row c is c itself, and every entry of row c lies within 256 clusters of c. Slots 0 to near_count[c] - 1 of row c of near_list are live; the other slots are ignored.
All inputs are finite; a program needn't handle non-finite values.
Results may differ from a plain program's by a relative error of at most 0.0056.
Values may be sent and summed in bfloat16 or wider, within the bound.
A program may use at most 128 MiB of HBM per device.

v0:
```python
import jax
import jax.numpy as jnp
from jax import lax
from jax.sharding import PartitionSpec as P

R = 8
U = 32
NBR = 8
K0 = 64
K1 = 1024
IL = 12


def passed_along(array, axis, by):
    size = lax.axis_size(axis)
    pairs = [(i, i + by) for i in range(size) if 0 <= i + by < size]
    return lax.ppermute(array, axis, pairs)


def product(pattern, left_side, right_side):
    return jnp.einsum(pattern, left_side, right_side, preferred_element_type=jnp.float32)


def complex_terms(pattern, left_side, right_side, conjugate):
    if conjugate:
        real_part = product(pattern, left_side[0], right_side[0]) + product(
            pattern, left_side[1], right_side[1]
        )
        imag_part = product(pattern, left_side[1], right_side[0]) - product(
            pattern, left_side[0], right_side[1]
        )
    else:
        real_part = product(pattern, left_side[0], right_side[0]) - product(
            pattern, left_side[1], right_side[1]
        )
        imag_part = product(pattern, left_side[1], right_side[0]) + product(
            pattern, left_side[0], right_side[1]
        )
    return jnp.stack([real_part, imag_part])


def aggregate(current_block, radiation_block, interp, shift_angle):
    leaf_pattern = complex_terms("rcu,cuq->rcq", current_block, radiation_block, False).astype(
        jnp.bfloat16
    )
    clusters_here = leaf_pattern.shape[2]
    upward = jnp.dot(
        leaf_pattern.reshape(2, R, clusters_here, 2, K0), interp, preferred_element_type=jnp.float32
    )
    upward = upward.reshape(2, R, clusters_here // 8, 8, 2, K1)
    cosine = jnp.cos(shift_angle)[:, None, :]
    sine_part = jnp.sin(shift_angle)[:, None, :]
    real_part = upward[0] * cosine - upward[1] * sine_part
    imag_part = upward[0] * sine_part + upward[1] * cosine
    summed = jnp.stack([real_part.sum(axis=2), imag_part.sum(axis=2)])
    return summed.reshape(2, R, clusters_here // 8, 2 * K1).astype(jnp.bfloat16)


def disaggregate(received, radiation_block, interp, shift_angle):
    boxes_here = received.shape[2]
    widened = received.astype(jnp.float32).reshape(2, R, boxes_here, 1, 2, K1)
    cosine = jnp.cos(shift_angle)[:, None, :]
    sine_part = jnp.sin(shift_angle)[:, None, :]
    real_part = widened[0] * cosine + widened[1] * sine_part
    imag_part = widened[1] * cosine - widened[0] * sine_part
    shifted = jnp.stack([real_part, imag_part]).astype(jnp.bfloat16)
    downward = jnp.dot(shifted, interp.T, preferred_element_type=jnp.float32).astype(jnp.bfloat16)
    downward = downward.reshape(2, R, boxes_here * 8, 2 * K0)
    return complex_terms("rcq,cuq->rcu", downward, radiation_block, True)


def local(
    currents,
    near_blocks,
    near_list,
    near_count,
    radiation,
    interp,
    shift_angle,
    translation,
    trans_box,
    trans_off,
):
    below_rows = passed_along(currents, ("grp", "smp"), 1)
    above_rows = passed_along(currents, ("grp", "smp"), -1)
    clusters_here = near_list.shape[0]
    extended = jnp.concatenate([below_rows, currents, above_rows], axis=2).reshape(
        2, R, 3 * clusters_here, U
    )
    extended_rows = extended.transpose(2, 0, 1, 3).reshape(3 * clusters_here, 2 * R * U)
    device = lax.axis_index(("grp", "smp"))
    local_index = near_list - (device * clusters_here - clusters_here)
    slots = jnp.arange(NBR, dtype=jnp.int32)
    live_mask = slots[None, :] < near_count[:, None]
    row_ids = jnp.arange(3 * clusters_here, dtype=jnp.int32)
    picker = jnp.logical_and(
        local_index[:, :, None] == row_ids[None, None, :], live_mask[:, :, None]
    )
    picker = picker.astype(jnp.bfloat16).reshape(clusters_here * NBR, 3 * clusters_here)
    gathered_near = jnp.dot(picker, extended_rows, preferred_element_type=jnp.float32).astype(
        jnp.bfloat16
    )
    gathered_near = gathered_near.reshape(clusters_here, NBR, 2, R, U).transpose(2, 3, 0, 1, 4)
    gathered_near = gathered_near.reshape(2, R, clusters_here, NBR * U)
    near_field = complex_terms("cum,rcm->rcu", near_blocks, gathered_near, False)
    current_grid = currents.reshape(2, R, clusters_here, U)
    box_pattern = aggregate(current_grid, radiation, interp, shift_angle)
    spread = lax.all_to_all(box_pattern, ("grp", "smp"), split_axis=3, concat_axis=2, tiled=True)
    all_boxes = spread.shape[2]
    samples_here = spread.shape[3]
    lane_width = R * samples_here
    box_rows = spread.transpose(0, 2, 1, 3).reshape(2, all_boxes, lane_width)
    box_real = box_rows[0]
    box_imag = box_rows[1]
    operator_rows = jnp.tile(translation, (1, 1, R))
    operator_real = operator_rows[0]
    operator_imag = operator_rows[1]

    def turn(column, totals):
        partners = lax.dynamic_slice_in_dim(trans_box, column, 1, 1)[:, 0]
        offsets = lax.dynamic_slice_in_dim(trans_off, column, 1, 1)[:, 0]
        part_real = jnp.take(box_real, partners, axis=0).astype(jnp.float32)
        part_imag = jnp.take(box_imag, partners, axis=0).astype(jnp.float32)
        oper_real = jnp.take(operator_real, offsets, axis=0).astype(jnp.float32)
        oper_imag = jnp.take(operator_imag, offsets, axis=0).astype(jnp.float32)
        real_total = totals[0] + oper_real * part_real - oper_imag * part_imag
        imag_total = totals[1] + oper_real * part_imag + oper_imag * part_real
        return (real_total, imag_total)

    empty = jnp.zeros((all_boxes, lane_width), jnp.float32)
    real_total, imag_total = lax.fori_loop(0, IL, turn, (empty, empty))
    translated = jnp.stack([real_total, imag_total]).astype(jnp.bfloat16)
    translated = translated.reshape(2, all_boxes, R, samples_here).transpose(0, 2, 1, 3)
    received = lax.all_to_all(translated, ("grp", "smp"), split_axis=2, concat_axis=3, tiled=True)
    far_field = disaggregate(received, radiation, interp, shift_angle)
    total = near_field + far_field
    return total.reshape(2, R, clusters_here * U)


def solution(mesh):
    placed = (
        P(None, None, ("grp", "smp")),
        P(None, ("grp", "smp"), None, None),
        P(("grp", "smp"), None),
        P(("grp", "smp")),
        P(None, ("grp", "smp"), None, None),
        P(),
        P(),
        P(None, None, ("grp", "smp")),
        P(),
        P(),
    )
    return jax.shard_map(
        local, mesh=mesh, in_specs=placed, out_specs=P(None, None, ("grp", "smp")), check_vma=False
    )
```

profile of v0, /device:TPU:1, one launch (start us, length us, event | category | flops | bytes accessed | tf_op | source)
XLA Modules:
  0.0 1151.7 jit_solution(8395502711888851384)
XLA Ops:
  30.9 16.7 %subtract_reduce_fusion = (bf16[8,32,2,1024]{3,1,2,0:T(8,128)(2,1)S(1)}, bf16[8,32,2,1024]{3,1,2,0:T(8,128)(2,1)S(1)}) fusion(f32[2,8,256,2,1024]{4,2,3,1,0:T(8,128)} %fusion.103, f32[8,1024]{1,0:T(8,128)S(1)} %get-tuple-element.282, f32[8,1024]{1,0:T(8,128)S(1)} %get-tuple-element.281), kind=kLoop, calls=%fused_computation.35 | loop fusion | flops 32505856 | bytes 35717120 | tf_op jit(solution)/shard_map/reduce_sum | solution.py:55
  154.2 795.8 %while.16 = (s32[]{:T(128)}, f32[4096,128]{1,0:T(8,128)}, f32[4096,128]{1,0:T(8,128)}, s32[4096,12]{0,1:T(8,128)}, s32[4096,12]{0,1:T(8,128)}, /*index=5*/bf16[4...) while((s32[]{:T(128)}, f32[4096,128]{1,0:T(8,128)}, ...), condition=%wide.region_3.6_spmd.clone, body=%wide.region_2.5_spmd.clone.sunk | while | flops 9519107 | bytes 21723004 | solution.py:131
  167.6 15.0 %gather_fusion.1 = bf16[4096,128]{1,0:T(8,128)(2,1)} fusion(bf16[316,128]{1,0:T(8,128)(2,1)S(1)} %copy.225, s32[4096]{0:T(1024)S(1)} %fusion.133), kind=kCustom, calls=%fused_computation.2.clone.clone.1 | custom fusion | bytes 2113536 | tf_op jit(solution)/shard_map/while/body/eval_jaxpr/jit(_take)/gather | solution.py:125
  182.7 15.0 %gather_fusion.2 = bf16[4096,128]{1,0:T(8,128)(2,1)} fusion(bf16[4096,128]{1,0:T(8,128)(2,1)S(1)} %get-tuple-element.375, s32[4096]{0:T(1024)S(1)} %fusion.134), kind=kCustom, calls=%fused_computation.1.clone.clone.1 | custom fusion | bytes 2113536 | tf_op jit(solution)/shard_map/while/body/eval_jaxpr/jit(_take)/gather | solution.py:122
  232.8 15.0 %gather_fusion.1 = bf16[4096,128]{1,0:T(8,128)(2,1)} fusion(bf16[316,128]{1,0:T(8,128)(2,1)S(1)} %copy.225, s32[4096]{0:T(1024)S(1)} %fusion.133), kind=kCustom, calls=%fused_computation.2.clone.clone.1 | custom fusion | bytes 2113536 | tf_op jit(solution)/shard_map/while/body/eval_jaxpr/jit(_take)/gather | solution.py:125
  262.9 15.0 %gather_fusion.3 = bf16[4096,128]{1,0:T(8,128)(2,1)} fusion(bf16[4096,128]{1,0:T(8,128)(2,1)S(1)} %get-tuple-element.376, s32[4096]{0:T(1024)S(1)} %fusion.134), kind=kCustom, calls=%fused_computation.3.clone.clone.1 | custom fusion | bytes 2113536 | tf_op jit(solution)/shard_map/while/body/eval_jaxpr/jit(_take)/gather | solution.py:123
  299.3 15.0 %gather_fusion.1 = bf16[4096,128]{1,0:T(8,128)(2,1)} fusion(bf16[316,128]{1,0:T(8,128)(2,1)S(1)} %copy.225, s32[4096]{0:T(1024)S(1)} %fusion.133), kind=kCustom, calls=%fused_computation.2.clone.clone.1 | custom fusion | bytes 2113536 | tf_op jit(solution)/shard_map/while/body/eval_jaxpr/jit(_take)/gather | solution.py:125
  314.3 15.0 %gather_fusion.2 = bf16[4096,128]{1,0:T(8,128)(2,1)} fusion(bf16[4096,128]{1,0:T(8,128)(2,1)S(1)} %get-tuple-element.375, s32[4096]{0:T(1024)S(1)} %fusion.134), kind=kCustom, calls=%fused_computation.1.clone.clone.1 | custom fusion | bytes 2113536 | tf_op jit(solution)/shard_map/while/body/eval_jaxpr/jit(_take)/gather | solution.py:122
  329.3 15.0 %gather_fusion.3 = bf16[4096,128]{1,0:T(8,128)(2,1)} fusion(bf16[4096,128]{1,0:T(8,128)(2,1)S(1)} %get-tuple-element.376, s32[4096]{0:T(1024)S(1)} %fusion.134), kind=kCustom, calls=%fused_computation.3.clone.clone.1 | custom fusion | bytes 2113536 | tf_op jit(solution)/shard_map/while/body/eval_jaxpr/jit(_take)/gather | solution.py:123
  365.7 15.0 %gather_fusion.1 = bf16[4096,128]{1,0:T(8,128)(2,1)} fusion(bf16[316,128]{1,0:T(8,128)(2,1)S(1)} %copy.225, s32[4096]{0:T(1024)S(1)} %fusion.133), kind=kCustom, calls=%fused_computation.2.clone.clone.1 | custom fusion | bytes 2113536 | tf_op jit(solution)/shard_map/while/body/eval_jaxpr/jit(_take)/gather | solution.py:125
  380.7 15.0 %gather_fusion.2 = bf16[4096,128]{1,0:T(8,128)(2,1)} fusion(bf16[4096,128]{1,0:T(8,128)(2,1)S(1)} %get-tuple-element.375, s32[4096]{0:T(1024)S(1)} %fusion.134), kind=kCustom, calls=%fused_computation.1.clone.clone.1 | custom fusion | bytes 2113536 | tf_op jit(solution)/shard_map/while/body/eval_jaxpr/jit(_take)/gather | solution.py:122
  432.1 15.0 %gather_fusion.1 = bf16[4096,128]{1,0:T(8,128)(2,1)} fusion(bf16[316,128]{1,0:T(8,128)(2,1)S(1)} %copy.225, s32[4096]{0:T(1024)S(1)} %fusion.133), kind=kCustom, calls=%fused_computation.2.clone.clone.1 | custom fusion | bytes 2113536 | tf_op jit(solution)/shard_map/while/body/eval_jaxpr/jit(_take)/gather | solution.py:125
  447.1 15.0 %gather_fusion.2 = bf16[4096,128]{1,0:T(8,128)(2,1)} fusion(bf16[4096,128]{1,0:T(8,128)(2,1)S(1)} %get-tuple-element.375, s32[4096]{0:T(1024)S(1)} %fusion.134), kind=kCustom, calls=%fused_computation.1.clone.clone.1 | custom fusion | bytes 2113536 | tf_op jit(solution)/shard_map/while/body/eval_jaxpr/jit(_take)/gather | solution.py:122
  462.1 15.0 %gather_fusion.3 = bf16[4096,128]{1,0:T(8,128)(2,1)} fusion(bf16[4096,128]{1,0:T(8,128)(2,1)S(1)} %get-tuple-element.376, s32[4096]{0:T(1024)S(1)} %fusion.134), kind=kCustom, calls=%fused_computation.3.clone.clone.1 | custom fusion | bytes 2113536 | tf_op jit(solution)/shard_map/while/body/eval_jaxpr/jit(_take)/gather | solution.py:123
  498.5 15.0 %gather_fusion.1 = bf16[4096,128]{1,0:T(8,128)(2,1)} fusion(bf16[316,128]{1,0:T(8,128)(2,1)S(1)} %copy.225, s32[4096]{0:T(1024)S(1)} %fusion.133), kind=kCustom, calls=%fused_computation.2.clone.clone.1 | custom fusion | bytes 2113536 | tf_op jit(solution)/shard_map/while/body/eval_jaxpr/jit(_take)/gather | solution.py:125
  513.5 15.0 %gather_fusion.2 = bf16[4096,128]{1,0:T(8,128)(2,1)} fusion(bf16[4096,128]{1,0:T(8,128)(2,1)S(1)} %get-tuple-element.375, s32[4096]{0:T(1024)S(1)} %fusion.134), kind=kCustom, calls=%fused_computation.1.clone.clone.1 | custom fusion | bytes 2113536 | tf_op jit(solution)/shard_map/while/body/eval_jaxpr/jit(_take)/gather | solution.py:122
  564.9 15.0 %gather_fusion.1 = bf16[4096,128]{1,0:T(8,128)(2,1)} fusion(bf16[316,128]{1,0:T(8,128)(2,1)S(1)} %copy.225, s32[4096]{0:T(1024)S(1)} %fusion.133), kind=kCustom, calls=%fused_computation.2.clone.clone.1 | custom fusion | bytes 2113536 | tf_op jit(solution)/shard_map/while/body/eval_jaxpr/jit(_take)/gather | solution.py:125
  580.0 15.0 %gather_fusion.2 = bf16[4096,128]{1,0:T(8,128)(2,1)} fusion(bf16[4096,128]{1,0:T(8,128)(2,1)S(1)} %get-tuple-element.375, s32[4096]{0:T(1024)S(1)} %fusion.134), kind=kCustom, calls=%fused_computation.1.clone.clone.1 | custom fusion | bytes 2113536 | tf_op jit(solution)/shard_map/while/body/eval_jaxpr/jit(_take)/gather | solution.py:122
  595.0 15.0 %gather_fusion.3 = bf16[4096,128]{1,0:T(8,128)(2,1)} fusion(bf16[4096,128]{1,0:T(8,128)(2,1)S(1)} %get-tuple-element.376, s32[4096]{0:T(1024)S(1)} %fusion.134), kind=kCustom, calls=%fused_computation.3.clone.clone.1 | custom fusion | bytes 2113536 | tf_op jit(solution)/shard_map/while/body/eval_jaxpr/jit(_take)/gather | solution.py:123
  631.4 15.0 %gather_fusion.1 = bf16[4096,128]{1,0:T(8,128)(2,1)} fusion(bf16[316,128]{1,0:T(8,128)(2,1)S(1)} %copy.225, s32[4096]{0:T(1024)S(1)} %fusion.133), kind=kCustom, calls=%fused_computation.2.clone.clone.1 | custom fusion | bytes 2113536 | tf_op jit(solution)/shard_map/while/body/eval_jaxpr/jit(_take)/gather | solution.py:125
  646.4 15.0 %gather_fusion.2 = bf16[4096,128]{1,0:T(8,128)(2,1)} fusion(bf16[4096,128]{1,0:T(8,128)(2,1)S(1)} %get-tuple-element.375, s32[4096]{0:T(1024)S(1)} %fusion.134), kind=kCustom, calls=%fused_computation.1.clone.clone.1 | custom fusion | bytes 2113536 | tf_op jit(solution)/shard_map/while/body/eval_jaxpr/jit(_take)/gather | solution.py:122
  697.8 15.0 %gather_fusion.1 = bf16[4096,128]{1,0:T(8,128)(2,1)} fusion(bf16[316,128]{1,0:T(8,128)(2,1)S(1)} %copy.225, s32[4096]{0:T(1024)S(1)} %fusion.133), kind=kCustom, calls=%fused_computation.2.clone.clone.1 | custom fusion | bytes 2113536 | tf_op jit(solution)/shard_map/while/body/eval_jaxpr/jit(_take)/gather | solution.py:125
  712.8 15.0 %gather_fusion.2 = bf16[4096,128]{1,0:T(8,128)(2,1)} fusion(bf16[4096,128]{1,0:T(8,128)(2,1)S(1)} %get-tuple-element.375, s32[4096]{0:T(1024)S(1)} %fusion.134), kind=kCustom, calls=%fused_computation.1.clone.clone.1 | custom fusion | bytes 2113536 | tf_op jit(solution)/shard_map/while/body/eval_jaxpr/jit(_take)/gather | solution.py:122
  764.2 15.0 %gather_fusion.1 = bf16[4096,128]{1,0:T(8,128)(2,1)} fusion(bf16[316,128]{1,0:T(8,128)(2,1)S(1)} %copy.225, s32[4096]{0:T(1024)S(1)} %fusion.133), kind=kCustom, calls=%fused_computation.2.clone.clone.1 | custom fusion | bytes 2113536 | tf_op jit(solution)/shard_map/while/body/eval_jaxpr/jit(_take)/gather | solution.py:125
  779.2 15.0 %gather_fusion.2 = bf16[4096,128]{1,0:T(8,128)(2,1)} fusion(bf16[4096,128]{1,0:T(8,128)(2,1)S(1)} %get-tuple-element.375, s32[4096]{0:T(1024)S(1)} %fusion.134), kind=kCustom, calls=%fused_computation.1.clone.clone.1 | custom fusion | bytes 2113536 | tf_op jit(solution)/shard_map/while/body/eval_jaxpr/jit(_take)/gather | solution.py:122
  830.6 15.0 %gather_fusion.1 = bf16[4096,128]{1,0:T(8,128)(2,1)} fusion(bf16[316,128]{1,0:T(8,128)(2,1)S(1)} %copy.225, s32[4096]{0:T(1024)S(1)} %fusion.133), kind=kCustom, calls=%fused_computation.2.clone.clone.1 | custom fusion | bytes 2113536 | tf_op jit(solution)/shard_map/while/body/eval_jaxpr/jit(_take)/gather | solution.py:125
  845.6 15.0 %gather_fusion.2 = bf16[4096,128]{1,0:T(8,128)(2,1)} fusion(bf16[4096,128]{1,0:T(8,128)(2,1)S(1)} %get-tuple-element.375, s32[4096]{0:T(1024)S(1)} %fusion.134), kind=kCustom, calls=%fused_computation.1.clone.clone.1 | custom fusion | bytes 2113536 | tf_op jit(solution)/shard_map/while/body/eval_jaxpr/jit(_take)/gather | solution.py:122
  897.0 15.0 %gather_fusion.1 = bf16[4096,128]{1,0:T(8,128)(2,1)} fusion(bf16[316,128]{1,0:T(8,128)(2,1)S(1)} %copy.225, s32[4096]{0:T(1024)S(1)} %fusion.133), kind=kCustom, calls=%fused_computation.2.clone.clone.1 | custom fusion | bytes 2113536 | tf_op jit(solution)/shard_map/while/body/eval_jaxpr/jit(_take)/gather | solution.py:125
  912.1 15.0 %gather_fusion.2 = bf16[4096,128]{1,0:T(8,128)(2,1)} fusion(bf16[4096,128]{1,0:T(8,128)(2,1)S(1)} %get-tuple-element.375, s32[4096]{0:T(1024)S(1)} %fusion.134), kind=kCustom, calls=%fused_computation.1.clone.clone.1 | custom fusion | bytes 2113536 | tf_op jit(solution)/shard_map/while/body/eval_jaxpr/jit(_take)/gather | solution.py:122
  969.2 23.2 %reshape.214 = bf16[128,2,4096]{2,1,0:T(2,128)(2,1)} reshape(bf16[4096,2,8,16]{3,2,1,0:T(8,128)(2,1)} %bitcast.151) | data formatting | bytes 4194304
  1032.2 18.6 %reshape.215 = bf16[4096,2,8,16]{3,2,1,0:T(8,128)(2,1)} reshape(bf16[128,2,4096]{2,1,0:T(2,128)(2,1)} %all-to-all-done.1) | data formatting | bytes 4194304
  1050.9 15.2 %copy.194 = bf16[2,8,4096,16]{2,3,1,0:T(8,128)(2,1)S(1)} copy(bf16[2,8,4096,16]{3,1,0,2:T(8,128)(2,1)} %bitcast.152) | data formatting | bytes 4194304 | tf_op jit(solution)/shard_map/all_to_all | solution.py:134
  (253 shorter events, 671.2 us)
Async XLA Ops:
  0.0 17.2 %copy-start = (bf16[64,1024]{1,0:T(8,128)(2,1)S(1)}, bf16[64,1024]{1,0:T(8,128)(2,1)}, u32[]{:S(2)}) copy-start(bf16[64,1024]{1,0:T(8,128)(2,1)} %param.21) | copy-start | bytes 393220
  0.0 86.8 %collective-permute-start = (bf16[2,8,8192]{2,1,0:T(8,128)(2,1)}, bf16[2,8,8192]{2,1,0:T(8,128)(2,1)}, u32[]{:S(2)}, u32[]{:S(2)}) collective-permute-start(bf16[2,8,8192]{2,1,0:T(8,128)(2,1)} %param.16), channel_id=1, source_target_pairs={{0,1},{1,2},{2,3},{3,4},{4,5},{5,6},{6,7},{7,8},{8,9},{9,10},{10,1... | collective-permute-start | bytes 786440 | tf_op jit(solution)/shard_map/ppermute | solution.py:17
  5.1 81.7 %collective-permute-start.1 = (bf16[2,8,8192]{2,1,0:T(8,128)(2,1)}, bf16[2,8,8192]{2,1,0:T(8,128)(2,1)}, u32[]{:S(2)}, u32[]{:S(2)}) collective-permute-start(bf16[2,8,8192]{2,1,0:T(8,128)(2,1)} %param.16), channel_id=1, source_target_pairs={{1,0},{2,1},{3,2},{4,3},{5,4},{6,5},{7,6},{8,7},{9,8},{10,9},{11,1... | collective-permute-start | bytes 786440 | tf_op jit(solution)/shard_map/ppermute | solution.py:17
  8.7 4.7 copy-start.2
  14.1 2.9 copy-start.10
  17.2 13.7 %copy-start.6 = (f32[8,1024]{1,0:T(8,128)}, f32[8,1024]{1,0:T(8,128)S(1)}, u32[]{:S(2)}) copy-start(f32[8,1024]{1,0:T(8,128)S(1)} %get-tuple-element.281) | copy-start | bytes 98308
  17.2 13.7 %copy-start.8 = (f32[8,1024]{1,0:T(8,128)}, f32[8,1024]{1,0:T(8,128)S(1)}, u32[]{:S(2)}) copy-start(f32[8,1024]{1,0:T(8,128)S(1)} %get-tuple-element.282) | copy-start | bytes 98308
  75.2 11.1 copy-start.13
  75.2 11.2 copy-start.12
  75.2 11.6 %copy-start.11 = (bf16[2,316,16]{1,2,0:T(8,128)(2,1)S(1)}, bf16[2,316,16]{1,2,0:T(8,128)(2,1)}, u32[]{:S(2)}) copy-start(bf16[2,316,16]{1,2,0:T(8,128)(2,1)} %param.23) | copy-start | bytes 60676
  75.2 11.6 %copy-start.5 = (bf16[2,8,8192]{2,1,0:T(8,128)(2,1)S(1)}, bf16[2,8,8192]{2,1,0:T(8,128)(2,1)}, u32[]{:S(2)}) copy-start(bf16[2,8,8192]{2,1,0:T(8,128)(2,1)} %param.16) | copy-start | bytes 786436
  75.2 41.0 %all-to-all-start = ((bf16[128,2,4096]{2,1,0:T(2,128)(2,1)}), bf16[128,2,4096]{2,1,0:T(2,128)(2,1)}, u32[]{:S(2)}, u32[]{:S(2)}) async-start(bf16[128,2,4096]{2,1,0:T(2,128)(2,1)} %reshape.212), calls=%async_computation | async-start | bytes 4194304 | tf_op jit(solution)/shard_map/all_to_all | solution.py:108
  950.0 2.2 copy-start.1
  992.5 39.8 %all-to-all-start.1 = ((bf16[128,2,4096]{2,1,0:T(2,128)(2,1)}), bf16[128,2,4096]{2,1,0:T(2,128)(2,1)}, u32[]{:S(2)}, u32[]{:S(2)}) async-start(bf16[128,2,4096]{2,1,0:T(2,128)(2,1)} %reshape.214), calls=%async_computation.1 | async-start | bytes 4194304 | tf_op jit(solution)/shard_map/all_to_all | solution.py:134
  1111.2 7.3 copy-start.7
  1111.2 7.3 copy-start.9
  1140.7 2.9 copy-start.3
  1147.1 3.5 copy-start.4
where the time goes:
time: 1160 us; the launch traced here: 1150 us
  local copies, waits for them, and re-layouts  933 us (80%)
  other arithmetic  124 us (11%)
  matrix products  58.1 us (5%)
  starting transfers between devices  23.7 us (2%)
    gather x12, local copies, waits for them, and re-layouts, turn(): oper_imag = jnp.take(operator_imag, offsets, axis=0).astype(jnp.float32)  180 us
    gather x12, local copies, waits for them, and re-layouts, turn(): part_real = jnp.take(box_real, partners, axis=0).astype(jnp.float32)  180 us
    gather x12, local copies, waits for them, and re-layouts, turn(): part_imag = jnp.take(box_imag, partners, axis=0).astype(jnp.float32)  180 us
    gather x12, local copies, waits for them, and re-layouts, turn(): oper_real = jnp.take(operator_real, offsets, axis=0).astype(jnp.float32)  146 us
    add x12, other arithmetic, turn(): imag_total = totals[1] + oper_real * part_imag + oper_imag * part_real  93.7 us
    unnamed x34, local copies, waits for them, and re-layouts  69.2 us
    dot_general x12, matrix products, product(): jnp.einsum(pattern, left_side, right_side, preferred_element_type=jnp.flo...  33.4 us
    slice x3, local copies, waits for them, and re-layouts, disaggregate(): real_part = widened[0] * cosine + widened[1] * sine_part  29.5 us
  transfers between devices with their start and end apart: 4, of which 1 were waited for; matrix products, arithmetic and copies ran while one was open for 11% of the time, Pallas kernels for 0%

commit v1 on v0

v1 whole, which is shorter than its diff:
```python
import functools
import itertools
import random

import jax
import jax.numpy as jnp
from jax import lax
from jax.experimental import pallas as pl
from jax.experimental.pallas import tpu as pltpu
from jax.sharding import PartitionSpec as P

R = 8
U = 32
NBR = 8
K0 = 64
K1 = 1024
IL = 12
NC = 256
OFFS = 316
OFFS_PAD = 320
BOXES = 32
CHIPS = 64
AXES = ("grp", "smp")
MESH_ID = pl.DeviceIdType.MESH
F32 = jnp.float32
BF16 = jnp.bfloat16
VMEM_SPEC = pl.BlockSpec(memory_space=pltpu.VMEM)
SMEM_SPEC = pl.BlockSpec(memory_space=pltpu.SMEM)


def far_first():
    steps = [s for s in itertools.product(range(4), repeat=3) if s != (0, 0, 0)]
    random.Random(1).shuffle(steps)
    return sorted(steps, key=lambda s: -sum(min(a, 4 - a) for a in s))


STEPS = far_first()


def place():
    x = lax.axis_index("grp")
    smp = lax.axis_index("smp")
    core = lax.rem(smp, 2)
    y = lax.div(smp, 8)
    z = lax.rem(lax.div(smp, 2), 4)
    return x, y, z, core


def dot(left, right):
    return lax.dot_general(left, right, (((1,), (0,)), ((), ())), preferred_element_type=F32)


def dot_t(left, right):
    return lax.dot_general(left, right, (((1,), (1,)), ((), ())), preferred_element_type=F32)


def lane_ids(shape):
    return lax.broadcasted_iota(jnp.int32, shape, 1)


def build_matrix(interp, angle, matrix, trig):
    trig[0:8, :] = jnp.cos(angle[...])
    trig[8:16, :] = jnp.sin(angle[...])
    for block in range(8):
        lanes = slice(block * 128, block * 128 + 128)
        table = interp[:, lanes].astype(F32)
        for i in range(8):
            cosine = (table * trig[i : i + 1, lanes]).astype(BF16)
            sine_part = (table * trig[8 + i : 9 + i, lanes]).astype(BF16)
            first = slice(i * 64, i * 64 + 64)
            second = slice(512 + i * 64, 512 + i * 64 + 64)
            matrix[first, block * 256 : block * 256 + 128] = cosine
            matrix[first, block * 256 + 128 : block * 256 + 256] = sine_part
            matrix[second, block * 256 : block * 256 + 128] = -sine_part
            matrix[second, block * 256 + 128 : block * 256 + 256] = cosine


def up_kernel(cur, rad, interp, angle, send, matrix, trig, leaf, packed):
    build_matrix(interp, angle, matrix, trig)
    own = lax.broadcasted_iota(jnp.int32, (128, 256), 0) // 16 == lane_ids((128, 256)) // U
    own = own.astype(F32).astype(BF16)

    def box(b, carry):
        tile = cur[:, pl.ds(pl.multiple_of(b * 256, 256), 256)]
        spread = jnp.concatenate([tile] * 8, axis=0) * own
        real = rad[0, pl.ds(b * 8, 8)].reshape(256, 128)
        imag = rad[1, pl.ds(b * 8, 8)].reshape(256, 128)
        by_real = dot(spread, real)
        by_imag = dot(spread, imag)
        for i in range(8):
            lo = slice(i * 16, i * 16 + 8)
            hi = slice(i * 16 + 8, i * 16 + 16)
            leaf[pl.ds(i * 256 + b, 8, stride=32), :] = by_real[lo] - by_imag[hi]
            leaf[pl.ds((8 + i) * 256 + b, 8, stride=32), :] = by_imag[lo] + by_real[hi]
        return carry

    lax.fori_loop(0, BOXES, box, 0, unroll=2)
    left = lane_ids((256, 128)) < 64
    for c in range(2):
        for m in range(4):
            first = leaf[(c * 8 + 2 * m) * 256 : (c * 8 + 2 * m + 1) * 256, :]
            second = leaf[(c * 8 + 2 * m + 1) * 256 : (c * 8 + 2 * m + 2) * 256, :]
            lanes = slice((c * 4 + m) * 128, (c * 4 + m + 1) * 128)
            packed[0, :, lanes] = jnp.where(left, first, pltpu.roll(second, 64, 1)).astype(BF16)
            packed[1, :, lanes] = jnp.where(left, pltpu.roll(first, 64, 1), second).astype(BF16)
    for p in range(2):
        for block in range(8):
            out = dot(packed[p], matrix[:, block * 256 : block * 256 + 256]).astype(BF16)
            for r in range(R):
                rows = slice(r * 32, r * 32 + 32)
                for c in range(2):
                    send[(p * 8 + block) * 8 + r, c] = out[rows, c * 128 : c * 128 + 128]


def upward(cur, rad, interp, angle):
    return pl.pallas_call(
        up_kernel,
        out_shape=jax.ShapeDtypeStruct((128, 2, BOXES, 128), BF16),
        in_specs=[VMEM_SPEC] * 4,
        out_specs=VMEM_SPEC,
        scratch_shapes=[
            pltpu.VMEM((1024, 2048), BF16),
            pltpu.VMEM((16, 1024), F32),
            pltpu.VMEM((16 * 256, 128), F32),
            pltpu.VMEM((2, 256, 1024), BF16),
        ],
        compiler_params=pltpu.CompilerParams(vmem_limit_bytes=40 << 20),
        name="upward",
    )(cur, rad, interp, angle)


def exchange_kernel(forward, send, rec, send_sems, recv_sems, pass_sems, take_sems, own_sem):
    x, y, z, core = place()
    chip = x * 16 + y * 4 + z
    sibling = (x, (y * 4 + z) * 2 + 1 - core)

    def target(step, sign):
        tx, ty, tz = [lax.rem(a + (4 + sign * s) % 4, 4) for a, s in zip((x, y, z), step)]
        return tx * 16 + ty * 4 + tz, (tx, (ty * 4 + tz) * 2 + core)

    def slot(at):
        return rec.at[2 * at + core] if forward else rec.at[at]

    barrier = pltpu.get_barrier_semaphore()
    for step in STEPS:
        pl.semaphore_signal(barrier, inc=1, device_id=target(step, 1)[1], device_id_type=MESH_ID)
    if forward:
        pl.semaphore_signal(barrier, inc=1, device_id=sibling, device_id_type=MESH_ID)
    pl.semaphore_wait(barrier, len(STEPS) + int(forward))
    copies = []
    for n, step in enumerate(STEPS):
        to, device = target(step, 1)
        copies.append(
            pltpu.make_async_remote_copy(
                src_ref=send.at[to],
                dst_ref=slot(chip),
                send_sem=send_sems.at[n],
                recv_sem=recv_sems.at[n],
                device_id=device,
                device_id_type=MESH_ID,
            )
        )
        copies[-1].start()
    own = pltpu.make_async_copy(send.at[chip], slot(chip), own_sem)
    own.start()
    own.wait()
    if not forward:
        for copy in copies:
            copy.wait()
        return

    passes = []
    for n in range(CHIPS):
        if n == 0:
            source = chip
        else:
            copies[n - 1].wait_recv()
            source = target(STEPS[n - 1], -1)[0]
        passes.append(
            pltpu.make_async_remote_copy(
                src_ref=rec.at[2 * source + core],
                dst_ref=rec.at[2 * source + core],
                send_sem=pass_sems.at[n],
                recv_sem=take_sems.at[n],
                device_id=sibling,
                device_id_type=MESH_ID,
            )
        )
        passes[-1].start()
    for n in range(CHIPS):
        if n > 0:
            copies[n - 1].wait_send()
        passes[n].wait_send()
        source = chip if n == 0 else target(STEPS[n - 1], -1)[0]
        other = rec.at[2 * source + 1 - core]
        pltpu.make_async_copy(other, other, take_sems.at[n]).wait()


def exchange(send, forward):
    return pl.pallas_call(
        functools.partial(exchange_kernel, forward),
        out_shape=jax.ShapeDtypeStruct((128 if forward else 64, 2, 2, BOXES, 128), BF16),
        in_specs=[VMEM_SPEC],
        out_specs=VMEM_SPEC,
        scratch_shapes=[pltpu.SemaphoreType.DMA((CHIPS,))] * 4 + [pltpu.SemaphoreType.DMA],
        compiler_params=pltpu.CompilerParams(
            collective_id=1 if forward else 2, has_side_effects=True, vmem_limit_bytes=40 << 20
        ),
        name="exchange_up" if forward else "exchange_down",
    )(send)


def near_kernel(below, cur, above, blocks, where, out, ext):
    step = pl.program_id(0)

    @pl.when(step == 0)
    def _():
        rows = lax.broadcasted_iota(jnp.int32, (128, 512), 0)
        columns = lane_ids((128, 512))
        copier = jnp.logical_and(rows // U == columns // 128, rows % U == columns % U)
        copier = copier.astype(F32).astype(BF16)
        for part, ref in enumerate((below, cur, above)):

            def fill(g, carry, part=part, ref=ref):
                start = pl.multiple_of(g * 2048, 2048)
                piece = ref[:, pl.ds(start, 2048)]
                stacked = jnp.concatenate([piece[:, k * 128 : k * 128 + 128] for k in range(16)], axis=0)
                wide = dot(stacked, copier).astype(BF16)
                for k in range(16):
                    for j in range(4):
                        row = pl.multiple_of((part * NC + g * 64 + k * 4 + j) * 16, 16)
                        ext[pl.ds(row, 16), :] = wide[k * 16 : k * 16 + 16, j * 128 : j * 128 + 128]
                return carry

            lax.fori_loop(0, 4, fill, 0)
        ext[3 * NC * 16 : 3 * NC * 16 + 16, :] = jnp.zeros((16, 128), BF16)

    masks = [(lane_ids((16, 128)) // U == k).astype(F32).astype(BF16) for k in range(4)]
    own = lane_ids((16, 256)) // U
    for b in range(4):
        gathered = []
        for i in range(8):
            halves = []
            for h in range(2):
                total = None
                for k in range(4):
                    row = where[(step * 4 + b) * 64 + i * 8 + h * 4 + k]
                    piece = ext[pl.ds(pl.multiple_of(row, 16), 16), :] * masks[k]
                    total = piece if total is None else total + piece
                halves.append(total)
            gathered.append(jnp.concatenate(halves, axis=1))
        stacked = jnp.concatenate(gathered, axis=0)
        sums = []
        for c in range(2):
            result = dot_t(stacked, blocks[c, b * 8 : b * 8 + 8].reshape(256, 256))
            total = jnp.zeros((16, 256), F32)
            for i in range(8):
                total = jnp.where(own == i, result[i * 16 : i * 16 + 16], total)
            sums.append(total)
        real, imag = sums
        lanes = slice(b * 256, b * 256 + 256)
        out[0:8, lanes] = real[0:8] - imag[8:16]
        out[8:16, lanes] = imag[0:8] + real[8:16]


def near_part(below, cur, above, blocks, where):
    return pl.pallas_call(
        near_kernel,
        grid=(8,),
        out_shape=jax.ShapeDtypeStruct((16, NC * U), F32),
        in_specs=[
            pl.BlockSpec((16, NC * U), lambda i: (0, 0)),
            pl.BlockSpec((16, NC * U), lambda i: (0, 0)),
            pl.BlockSpec((16, NC * U), lambda i: (0, 0)),
            pl.BlockSpec((2, 32, U, NBR * U), lambda i: (0, i, 0, 0)),
            SMEM_SPEC,
        ],
        out_specs=pl.BlockSpec((16, 1024), lambda i: (0, i)),
        scratch_shapes=[pltpu.VMEM((3 * NC * 16 + 16, 128), BF16)],
        compiler_params=pltpu.CompilerParams(vmem_limit_bytes=40 << 20),
        cost_estimate=pl.CostEstimate(flops=600_000_000, bytes_accessed=9_000_000, transcendentals=0),
        name="near",
    )(below, cur, above, blocks, where)


def translate_kernel(rec, oper, which_box, which_off, out, field, table, sums):
    for k in range(8):
        table[pl.ds(k, OFFS_PAD, stride=8), :] = oper[k // 4]

    def widen(device, carry):
        for k in range(4):
            value = rec[device, k // 2, k % 2].astype(F32)
            field[pl.ds(device * 256 + k, 32, stride=8), :] = value
            field[pl.ds(device * 256 + k + 4, 32, stride=8), :] = value
        return carry

    lax.fori_loop(0, 128, widen, 0)

    def chunk(chip, carry):
        base = chip * (BOXES * IL)
        for b in range(BOXES):
            total = None
            for j in range(IL):
                row = pl.multiple_of(which_box[base + b * IL + j], 8)
                operator = pl.multiple_of(which_off[base + b * IL + j], 8)
                term = field[pl.ds(row, 8), :] * table[pl.ds(operator, 8), :]
                total = term if total is None else total + term
            sums[b * 8 : b * 8 + 8, :] = total
        parts = [sums[pl.ds(k, BOXES, stride=8), :] for k in range(8)]
        out[chip, 0, 0] = (parts[0] - parts[5]).astype(BF16)
        out[chip, 0, 1] = (parts[1] + parts[4]).astype(BF16)
        out[chip, 1, 0] = (parts[2] - parts[7]).astype(BF16)
        out[chip, 1, 1] = (parts[3] + parts[6]).astype(BF16)
        return carry

    lax.fori_loop(0, CHIPS, chunk, 0)


def translate(rec, oper, which_box, which_off):
    return pl.pallas_call(
        translate_kernel,
        out_shape=jax.ShapeDtypeStruct((CHIPS, 2, 2, BOXES, 128), BF16),
        in_specs=[VMEM_SPEC, VMEM_SPEC, SMEM_SPEC, SMEM_SPEC],
        out_specs=VMEM_SPEC,
        scratch_shapes=[
            pltpu.VMEM((4096 * 8, 128), F32),
            pltpu.VMEM((OFFS_PAD * 8, 128), F32),
            pltpu.VMEM((BOXES * 8, 128), F32),
        ],
        compiler_params=pltpu.CompilerParams(vmem_limit_bytes=40 << 20),
        name="translate",
    )(rec, oper, which_box, which_off)


def down_kernel(rec, rad, interp, angle, near, out, matrix, trig, leaf):
    build_matrix(interp, angle, matrix, trig)
    left = lane_ids((256, 128)) < 64
    for c in range(2):
        for half in range(2):
            rows = slice(c * 512 + half * 256, c * 512 + half * 256 + 256)
            results = []
            for p in range(2):
                pieces = []
                for block in range(8):
                    for c2 in range(2):
                        at = (p * 8 + block) * 8
                        pieces.append(rec[at : at + 8, c2].reshape(256, 128))
                fields = jnp.concatenate(pieces, axis=1)
                results.append(dot_t(fields, matrix[rows, :]))
            for m in range(2):
                first = results[0][:, m * 128 : m * 128 + 128]
                second = results[1][:, m * 128 : m * 128 + 128]
                at = (c * 8 + half * 4 + m * 2) * 256
                leaf[at : at + 256, :] = jnp.where(left, first, pltpu.roll(second, 64, 1))
                leaf[at + 256 : at + 512, :] = jnp.where(left, pltpu.roll(first, 64, 1), second)
    own = lane_ids((16, 256)) // U

    def box(b, carry):
        pieces = []
        for i in range(8):
            for c in range(2):
                pieces.append(leaf[pl.ds((c * 8 + i) * 256 + b, 8, stride=32), :])
        stacked = jnp.concatenate(pieces, axis=0).astype(BF16)
        sums = []
        for c in range(2):
            result = dot_t(stacked, rad[c, pl.ds(b * 8, 8)].reshape(256, 128))
            total = jnp.zeros((16, 256), F32)
            for i in range(8):
                total = jnp.where(own == i, result[i * 16 : i * 16 + 16], total)
            sums.append(total)
        real, imag = sums
        lanes = pl.ds(pl.multiple_of(b * 256, 256), 256)
        out[0:8, lanes] = near[0:8, lanes] + (real[0:8] + imag[8:16])
        out[8:16, lanes] = near[8:16, lanes] + (real[8:16] - imag[0:8])
        return carry

    lax.fori_loop(0, BOXES, box, 0, unroll=2)


def downward(rec, rad, interp, angle, near):
    return pl.pallas_call(
        down_kernel,
        out_shape=jax.ShapeDtypeStruct((16, NC * U), F32),
        in_specs=[VMEM_SPEC] * 5,
        out_specs=VMEM_SPEC,
        scratch_shapes=[
            pltpu.VMEM((1024, 2048), BF16),
            pltpu.VMEM((16, 1024), F32),
            pltpu.VMEM((16 * 256, 128), F32),
        ],
        compiler_params=pltpu.CompilerParams(vmem_limit_bytes=40 << 20),
        name="downward",
    )(rec, rad, interp, angle, near)


def passed_along(array, by):
    size = lax.axis_size(AXES)
    pairs = [(i, i + by) for i in range(size) if 0 <= i + by < size]
    return lax.ppermute(array, AXES, pairs)


def local(
    currents,
    near_blocks,
    near_list,
    near_count,
    radiation,
    interp,
    shift_angle,
    translation,
    trans_box,
    trans_off,
):
    device = lax.axis_index(AXES)
    core = lax.rem(device, 2)
    cur = currents.reshape(16, NC * U)
    below = passed_along(cur, 1)
    above = passed_along(cur, -1)
    groups = [list(range(8 * g, 8 * g + 8)) for g in range(4)]
    oper = lax.all_gather(translation, "smp", axis_index_groups=groups, axis=2, tiled=True)
    oper = jnp.pad(oper.astype(F32), ((0, 0), (0, OFFS_PAD - OFFS), (0, 0)))

    slots = jnp.arange(NBR, dtype=jnp.int32)
    row = near_list - (device * NC - NC)
    where = jnp.where(slots[None, :] < near_count[:, None], row, 3 * NC)
    where = (where * 16).reshape(NC * NBR)
    which_box = lax.dynamic_index_in_dim(trans_box.reshape(CHIPS, 2, BOXES * IL), core, 1, False)
    which_off = lax.dynamic_index_in_dim(trans_off.reshape(CHIPS, 2, BOXES * IL), core, 1, False)
    which_box = (which_box * 8).reshape(CHIPS * BOXES * IL)
    which_off = (which_off * 8).reshape(CHIPS * BOXES * IL)

    sent = upward(cur, radiation, interp, shift_angle)
    spread = exchange(sent.reshape(CHIPS, 2, 2, BOXES, 128), True)
    near = near_part(below, cur, above, near_blocks, where)
    translated = translate(spread, oper, which_box, which_off)
    received = exchange(translated, False)
    out = downward(received.reshape(128, 2, BOXES, 128), radiation, interp, shift_angle, near)
    return out.reshape(2, R, NC * U)


def solution(mesh):
    placed = (
        P(None, None, AXES),
        P(None, AXES, None, None),
        P(AXES, None),
        P(AXES),
        P(None, AXES, None, None),
        P(),
        P(),
        P(None, None, AXES),
        P(),
        P(),
    )
    return jax.shard_map(
        local, mesh=mesh, in_specs=placed, out_specs=P(None, None, AXES), check_vma=False
    )
```

time: 1160 us -> 169 us (0.15)
  local copies, waits for them, and re-layouts: 933 us -> 12.1 us
  Pallas kernels: 0 us -> 135 us
  other arithmetic: 124 us -> 0.24 us
  matrix products: 58.1 us -> 0 us
  starting transfers between devices: 23.7 us -> 6.85 us
  blocking collectives: 0 us -> 14.2 us
    gather x48 -> x0, local copies, waits for them, and re-layouts: 686 us -> none  [the longest x12 180 us: turn(): oper_imag = jnp.take(operator_imag, offsets, axis=0).astype(jnp.float32)]
    pallas_call x0 -> x6, Pallas kernels: none -> 135 us  [the longest x2 70.7 us: exchange(): pl.pallas_call(functools.partial(exchange_kernel, forward), out_shape=jax...]
    add x13 -> x0, other arithmetic: 94.5 us -> none  [the longest x12 93.7 us: turn(): imag_total = totals[1] + oper_real * part_imag + oper_imag * part_real]
    unnamed x34 -> x23, local copies, waits for them, and re-layouts: 69.2 us -> 7.87 us
    dot_general x15 -> x0, matrix products: 58.1 us -> none  [the longest x12 33.4 us: product(): jnp.einsum(pattern, left_side, right_side, preferred_element_type=jnp.flo...]
    slice x10 -> x0, local copies, waits for them, and re-layouts: 48.5 us -> none  [the longest x3 29.5 us: disaggregate(): real_part = widened[0] * cosine + widened[1] * sine_part]
    all_to_all x3 -> x0, local copies, waits for them, and re-layouts: 37.8 us -> none  [the longest x2 22.6 us: local(): lax.all_to_all(box_pattern, ('grp', 'smp'), split_axis=3, concat_axis=2,...]
    another operation x57 -> x0, local copies, waits for them, and re-layouts: 19.1 us -> none  [the longest x3 11.1 us: aggregate(): summed = jnp.stack([real_part.sum(axis=2), imag_part.sum(axis=2)])]
  transfers between devices with their start and end apart: 4 -> 2, of which waited for: 1 -> 0; matrix products, arithmetic and copies ran while one was open for 11% -> 4% of each run, Pallas kernels for 0% -> 71%
where the time goes in v1:
time: 169 us
  Pallas kernels  135 us (80%)
  blocking collectives  14.2 us (8%)
  local copies, waits for them, and re-layouts  12.1 us (7%)
  starting transfers between devices  6.85 us (4%)
    pallas_call x2, Pallas kernels, exchange(): pl.pallas_call(functools.partial(exchange_kernel, forward), out_shape=jax...  70.7 us
    pallas_call x1, Pallas kernels, translate(): pl.pallas_call(translate_kernel, out_shape=jax.ShapeDtypeStruct((CHIPS, 2...  40.7 us
    all_gather x1, blocking collectives, local(): lax.all_gather(translation, 'smp', axis_index_groups=groups, axis=2, tile...  14.2 us
    pallas_call x1, Pallas kernels, near_part(): pl.pallas_call(near_kernel, grid=(8,), out_shape=jax.ShapeDtypeStruct((16...  8.08 us
    pallas_call x1, Pallas kernels, upward(): pl.pallas_call(up_kernel, out_shape=jax.ShapeDtypeStruct((128, 2, BOXES,...  7.9 us
    unnamed x23, local copies, waits for them, and re-layouts  7.87 us
    pallas_call x1, Pallas kernels, downward(): pl.pallas_call(down_kernel, out_shape=jax.ShapeDtypeStruct((16, NC * U),...  7.81 us
    ppermute x2, starting transfers between devices, passed_along(): return lax.ppermute(array, AXES, pairs)  6.85 us
  transfers between devices with their start and end apart: 2, of which 0 were waited for; matrix products, arithmetic and copies ran while one was open for 4% of the time, Pallas kernels for 71%

profile of v1, /device:TPU:1, one launch (start us, length us, event | category | flops | bytes accessed | tf_op | source)
XLA Modules:
  0.0 168.9 jit_solution(16581291323910624888)
XLA Ops:
  0.0 4.9 %collective-permute-start = (bf16[16,8192]{1,0:T(8,128)(2,1)}, bf16[16,8192]{1,0:T(8,128)(2,1)S(1)}, u32[]{:S(2)}, u32[]{:S(2)}) collective-permute-start(bf16[16,8192]{1,0:T(8,128)(2,1)} %bitcast.8), channel_id=1, source_target_pairs={{0,1},{1,2},{2,3},{3,4},{4,5},{5,6},{6,7},{7,8},{8,9},{9,10},{10,1... | collective-permute-start | bytes 786440 | tf_op jit(solution)/shard_map/ppermute | solution.py:399
  4.9 1.9 %collective-permute-start.1 = (bf16[16,8192]{1,0:T(8,128)(2,1)}, bf16[16,8192]{1,0:T(8,128)(2,1)S(1)}, u32[]{:S(2)}, u32[]{:S(2)}) collective-permute-start(bf16[16,8192]{1,0:T(8,128)(2,1)} %bitcast.9), channel_id=1, source_target_pairs={{1,0},{2,1},{3,2},{4,3},{5,4},{6,5},{7,6},{8,7},{9,8},{10,9},{11,1... | collective-permute-start | bytes 786440 | tf_op jit(solution)/shard_map/ppermute | solution.py:399
  6.9 0.0 copy-start.6
  6.9 1.6 copy.18
  8.5 1.9 %reshape.32 = s32[64,2,384]{2,1,0:T(2,128)S(1)} reshape(s32[4096,12]{1,0:T(8,128)S(1)} %copy.18) | data formatting | bytes 393216 | tf_op jit(solution)/shard_map/reshape | solution.py:427
  10.4 0.0 copy-done.6
  10.4 0.0 copy-start.7
  10.4 0.6 copy.19
  11.1 0.0 copy-start.3
  11.1 0.0 copy-start.4
  11.1 0.0 copy-start.5
  11.1 1.9 %reshape.33 = s32[64,2,384]{2,1,0:T(2,128)S(1)} reshape(s32[4096,12]{1,0:T(8,128)S(1)} %copy.19) | data formatting | bytes 393216 | tf_op jit(solution)/shard_map/reshape | solution.py:428
  13.0 0.0 copy-done.7
  13.1 14.2 %all_gather.3 = bf16[2,316,128]{1,0,2:T(2,128)(2,1)S(1)} all-gather(bf16[2,316,16]{1,0,2:T(2,128)(2,1)S(1)} %copy.16), channel_id=1, replica_groups={{0,1,2,3,4,5,6,7},{8,9,10,11,12,13,14,15},{16,17,18,19,20,21,22,23},{24..., dimensions={2}, use_global_device_ids=true | all-gather | bytes 182016 | tf_op jit(solution)/shard_map/all_gather | solution.py:420
  27.3 0.2 copy.17
  27.5 0.2 dynamic-slice_multiply_fusion
  27.8 0.0 copy-start
  27.8 2.2 %copy-done = bf16[2,256,32,128]{3,2,1,0:T(8,128)(2,1)S(1)} copy-done((bf16[2,256,32,128]{3,2,1,0:T(8,128)(2,1)S(1)}, bf16[2,256,32,128]{3,2,1,0:T(8,128)(2,1)}, u32[]{:S(2)}) %copy-start) | copy-done | bytes 4194328
  30.0 7.9 %upward.1 = bf16[128,2,32,128]{3,2,1,0:T(8,128)(2,1)S(1)} custom-call(bf16[16,8192]{1,0:T(8,128)(2,1)S(1)} %bitcast.10, bf16[2,256,32,128]{3,2,1,0:T(8,128)(2,1)S(1)} %copy-done, bf16[64,1024]{1,0:T(8,128)(2,1)S(1)} %copy-done.4, f32[8,1024]{1,0:T(8,128)S(1)} %copy-done.5), custom_call_target="tpu_custom_call" | custom-call | tf_op jit(solution)/shard_map/upward/pallas_call | solution.py:116
  37.9 38.7 %exchange_up.1.rec = bf16[128,2,2,32,128]{4,3,2,1,0:T(8,128)(2,1)S(1)} custom-call(bf16[64,2,2,32,128]{4,3,2,1,0:T(8,128)(2,1)S(1)} %bitcast.6), custom_call_target="tpu_custom_call" | custom-call | tf_op jit(solution)/shard_map/exchange_up/pallas_call | solution.py:200
  76.6 40.7 %translate.1.send = bf16[64,2,2,32,128]{4,3,2,1,0:T(8,128)(2,1)S(1)} custom-call(bf16[128,2,2,32,128]{4,3,2,1,0:T(8,128)(2,1)S(1)} %exchange_up.1.rec, f32[2,320,128]{2,1,0:T(8,128)S(1)} %pad_convert_fusion.oper, s32[24576]{0:T(1024)S(1)} %bitcast.13, s32[24576]{0:T(1024)S(1)} %bitcast.12), custom_call_target="tpu_custom_call" | custom-call | tf_op jit(solution)/shard_map/translate/pallas_call | solution.py:320
  117.3 0.0 copy-start.8
  117.3 0.0 copy-start.9
  117.3 31.9 %exchange_down.1 = bf16[64,2,2,32,128]{4,3,2,1,0:T(8,128)(2,1)S(1)} custom-call(bf16[64,2,2,32,128]{4,3,2,1,0:T(8,128)(2,1)S(1)} %translate.1.send), custom_call_target="tpu_custom_call" | custom-call | tf_op jit(solution)/shard_map/exchange_down/pallas_call | solution.py:200
  149.3 0.1 copy.20
  149.4 0.1 reshape.35.where
  149.5 0.0 collective-permute-done.below
  149.6 0.0 collective-permute-done.1.above
  149.6 0.0 copy-start.2
  149.6 3.4 %copy-done.2 = bf16[2,256,32,256]{3,2,1,0:T(8,128)(2,1)S(1)} copy-done((bf16[2,256,32,256]{3,2,1,0:T(8,128)(2,1)S(1)}, bf16[2,256,32,256]{3,2,1,0:T(8,128)(2,1)}, u32[]{:S(2)}) %copy-start.2) | copy-done | bytes 8388632
  152.9 8.1 %near.1 = f32[16,8192]{1,0:T(8,128)S(1)} custom-call(bf16[16,8192]{1,0:T(8,128)(2,1)S(1)} %collective-permute-done.below, bf16[16,8192]{1,0:T(8,128)(2,1)S(1)} %bitcast.11, bf16[16,8192]{1,0:T(8,128)(2,1)S(1)} %collective-permute-done.1.above, bf16[2,256,32,256]{3,2,1,0:T(8,128)(2,1)S(1)} %copy-done.2, s32[2048]{0:T(1024)S(1)} %reshape.35.where), custom_call_target="tpu_custom_call" | custom-call | flops 600000000 | bytes 9000000 | tf_op jit(solution)/shard_map/near/pallas_call | solution.py:267
  161.0 7.8 %downward.1 = f32[16,8192]{1,0:T(8,128)} custom-call(bf16[128,2,32,128]{3,2,1,0:T(8,128)(2,1)S(1)} %bitcast.7, bf16[2,256,32,128]{3,2,1,0:T(8,128)(2,1)S(1)} %copy-done.1, bf16[64,1024]{1,0:T(8,128)(2,1)S(1)} %copy-done.4, f32[8,1024]{1,0:T(8,128)S(1)} %copy-done.5, f32[16,8192]{1,0:T(8,128)S(1)} %near.1), custom_call_target="tpu_custom_call" | custom-call | tf_op jit(solution)/shard_map/downward/pallas_call | solution.py:381
  (10 shorter events, 0.1 us)
Async XLA Ops:
  0.0 149.5 %collective-permute-start = (bf16[16,8192]{1,0:T(8,128)(2,1)}, bf16[16,8192]{1,0:T(8,128)(2,1)S(1)}, u32[]{:S(2)}, u32[]{:S(2)}) collective-permute-start(bf16[16,8192]{1,0:T(8,128)(2,1)} %bitcast.8), channel_id=1, source_target_pairs={{0,1},{1,2},{2,3},{3,4},{4,5},{5,6},{6,7},{7,8},{8,9},{9,10},{10,1... | collective-permute-start | bytes 786440 | tf_op jit(solution)/shard_map/ppermute | solution.py:399
  4.9 144.6 %collective-permute-start.1 = (bf16[16,8192]{1,0:T(8,128)(2,1)}, bf16[16,8192]{1,0:T(8,128)(2,1)S(1)}, u32[]{:S(2)}, u32[]{:S(2)}) collective-permute-start(bf16[16,8192]{1,0:T(8,128)(2,1)} %bitcast.9), channel_id=1, source_target_pairs={{1,0},{2,1},{3,2},{4,3},{5,4},{6,5},{7,6},{8,7},{9,8},{10,9},{11,1... | collective-permute-start | bytes 786440 | tf_op jit(solution)/shard_map/ppermute | solution.py:399
  6.9 3.5 %copy-start.6 = (s32[4096,12]{0,1:T(8,128)S(1)}, s32[4096,12]{0,1:T(8,128)}, u32[]{:S(2)}) copy-start(s32[4096,12]{0,1:T(8,128)} %param.19) | copy-start | bytes 589828
  10.4 2.6 %copy-start.7 = (bf16[2,316,16]{1,2,0:T(8,128)(2,1)S(1)}, bf16[2,316,16]{1,2,0:T(8,128)(2,1)}, u32[]{:S(2)}) copy-start(bf16[2,316,16]{1,2,0:T(8,128)(2,1)} %param.17) | copy-start | bytes 60676
  11.1 16.7 %copy-start.3 = (bf16[2,8,8192]{2,1,0:T(8,128)(2,1)S(1)}, bf16[2,8,8192]{2,1,0:T(8,128)(2,1)}, u32[]{:S(2)}) copy-start(bf16[2,8,8192]{2,1,0:T(8,128)(2,1)} %param.10) | copy-start | bytes 786436
  11.1 16.7 %copy-start.4 = (bf16[64,1024]{1,0:T(8,128)(2,1)S(1)}, bf16[64,1024]{1,0:T(8,128)(2,1)}, u32[]{:S(2)}) copy-start(bf16[64,1024]{1,0:T(8,128)(2,1)} %interp.3) | copy-start | bytes 393220
  11.1 16.7 %copy-start.5 = (f32[8,1024]{1,0:T(8,128)S(1)}, f32[8,1024]{1,0:T(8,128)}, u32[]{:S(2)}) copy-start(f32[8,1024]{1,0:T(8,128)} %angle.3) | copy-start | bytes 98308
  27.8 2.2 %copy-start = (bf16[2,256,32,128]{3,2,1,0:T(8,128)(2,1)S(1)}, bf16[2,256,32,128]{3,2,1,0:T(8,128)(2,1)}, u32[]{:S(2)}) copy-start(bf16[2,256,32,128]{3,2,1,0:T(8,128)(2,1)} %rad.3) | copy-start | bytes 12582916
  117.3 32.0 %copy-start.8 = (s32[256,8]{0,1:T(8,128)S(1)}, s32[256,8]{0,1:T(8,128)}, u32[]{:S(2)}) copy-start(s32[256,8]{0,1:T(8,128)} %param.12) | copy-start | bytes 24580
  117.3 32.0 %copy-start.9 = (s32[256]{0:T(256)S(1)}, s32[256]{0:T(256)}, u32[]{:S(2)}) copy-start(s32[256]{0:T(256)} %param.13) | copy-start | bytes 3076
  149.6 3.4 %copy-start.2 = (bf16[2,256,32,256]{3,2,1,0:T(8,128)(2,1)S(1)}, bf16[2,256,32,256]{3,2,1,0:T(8,128)(2,1)}, u32[]{:S(2)}) copy-start(bf16[2,256,32,256]{3,2,1,0:T(8,128)(2,1)} %blocks.1) | copy-start | bytes 25165828
  152.9 8.1 %copy-start.1 = (bf16[2,256,32,128]{3,2,1,0:T(8,128)(2,1)S(1)}, bf16[2,256,32,128]{3,2,1,0:T(8,128)(2,1)}, u32[]{:S(2)}) copy-start(bf16[2,256,32,128]{3,2,1,0:T(8,128)(2,1)} %rad.3) | copy-start | bytes 12582916

commit v2 on v1

v2 whole, which is shorter than its diff:
```python
import jax
import jax.numpy as jnp
from jax import lax
from jax.experimental import pallas as pl
from jax.experimental.pallas import tpu as pltpu
from jax.sharding import PartitionSpec as P

R = 8
U = 32
NBR = 8
K0 = 64
K1 = 1024
IL = 12
NC = 256
OFFS = 316
BOXES = 32
CHIPS = 64
AXES = ("grp", "smp")
MESH_ID = pl.DeviceIdType.MESH
F32 = jnp.float32
BF16 = jnp.bfloat16
VMEM_SPEC = pl.BlockSpec(memory_space=pltpu.VMEM)
SMEM_SPEC = pl.BlockSpec(memory_space=pltpu.SMEM)


def place():
    x = lax.axis_index("grp")
    smp = lax.axis_index("smp")
    core = lax.rem(smp, 2)
    y = lax.div(smp, 8)
    z = lax.rem(lax.div(smp, 2), 4)
    return x, y, z, core


def dot(left, right):
    return lax.dot_general(left, right, (((1,), (0,)), ((), ())), preferred_element_type=F32)


def dot_t(left, right):
    return lax.dot_general(left, right, (((1,), (1,)), ((), ())), preferred_element_type=F32)


def lane_ids(shape):
    return lax.broadcasted_iota(jnp.int32, shape, 1)


def build_matrix(interp, trig, matrix):
    for block in range(8):
        lanes = slice(block * 128, block * 128 + 128)
        table = interp[:, lanes].astype(F32)
        for i in range(8):
            cosine = (table * trig[i : i + 1, lanes]).astype(BF16)
            sine_part = (table * trig[8 + i : 9 + i, lanes]).astype(BF16)
            first = slice(i * 64, i * 64 + 64)
            second = slice(512 + i * 64, 512 + i * 64 + 64)
            matrix[first, block * 256 : block * 256 + 128] = cosine
            matrix[first, block * 256 + 128 : block * 256 + 256] = sine_part
            matrix[second, block * 256 : block * 256 + 128] = -sine_part
            matrix[second, block * 256 + 128 : block * 256 + 256] = cosine


def leaf_patterns(cur, rad, leaf):
    own = lax.broadcasted_iota(jnp.int32, (128, 256), 0) // 16 == lane_ids((128, 256)) // U
    own = own.astype(F32).astype(BF16)

    def box(b, carry):
        tile = cur[:, pl.ds(pl.multiple_of(b * 256, 256), 256)]
        spread = jnp.concatenate([tile] * 8, axis=0) * own
        real = rad[0, pl.ds(b * 8, 8)].reshape(256, 128)
        imag = rad[1, pl.ds(b * 8, 8)].reshape(256, 128)
        by_real = dot(spread, real)
        by_imag = dot(spread, imag)
        for i in range(8):
            lo = slice(i * 16, i * 16 + 8)
            hi = slice(i * 16 + 8, i * 16 + 16)
            leaf[pl.ds(i * 256 + b, 8, stride=32), :] = by_real[lo] - by_imag[hi]
            leaf[pl.ds((8 + i) * 256 + b, 8, stride=32), :] = by_imag[lo] + by_real[hi]
        return carry

    lax.fori_loop(0, BOXES, box, 0, unroll=2)


def pack_leaves(leaf, packed):
    left = lane_ids((256, 128)) < 64
    for c in range(2):
        for m in range(4):
            first = leaf[(c * 8 + 2 * m) * 256 : (c * 8 + 2 * m + 1) * 256, :]
            second = leaf[(c * 8 + 2 * m + 1) * 256 : (c * 8 + 2 * m + 2) * 256, :]
            lanes = slice((c * 4 + m) * 128, (c * 4 + m + 1) * 128)
            packed[0, :, lanes] = jnp.where(left, first, pltpu.roll(second, 64, 1)).astype(BF16)
            packed[1, :, lanes] = jnp.where(left, pltpu.roll(first, 64, 1), second).astype(BF16)


def spread_currents(window, part, ext):
    rows = lax.broadcasted_iota(jnp.int32, (128, 512), 0)
    columns = lane_ids((128, 512))
    copier = jnp.logical_and(rows // U == columns // 128, rows % U == columns % U)
    copier = copier.astype(F32).astype(BF16)

    def fill(g, carry):
        piece = window[part, :, pl.ds(pl.multiple_of(g * 2048, 2048), 2048)]
        stacked = jnp.concatenate([piece[:, k * 128 : k * 128 + 128] for k in range(16)], axis=0)
        wide = dot(stacked, copier).astype(BF16)
        for k in range(16):
            for j in range(4):
                row = part * NC + g * 64 + k * 4 + j
                ext[row] = wide[k * 16 : k * 16 + 16, j * 128 : j * 128 + 128]
        return carry

    lax.fori_loop(0, 4, fill, 0)


def near_box(b, blocks, where, ext, out):
    masks = [(lane_ids((16, 128)) // U == k).astype(F32).astype(BF16) for k in range(4)]
    own = lane_ids((16, 256)) // U
    gathered = []
    for i in range(8):
        halves = []
        for h in range(2):
            total = None
            for k in range(4):
                row = where[(h * 4 + k) * NC + b * 8 + i]
                piece = ext[row] * masks[k]
                total = piece if total is None else total + piece
            halves.append(total)
        gathered.append(jnp.concatenate(halves, axis=1))
    stacked = jnp.concatenate(gathered, axis=0)
    sums = []
    for c in range(2):
        result = dot_t(stacked, blocks[c, pl.ds(b * 8, 8)].reshape(256, 256))
        total = jnp.zeros((16, 256), F32)
        for i in range(8):
            total = jnp.where(own == i, result[i * 16 : i * 16 + 16], total)
        sums.append(total)
    real, imag = sums
    lanes = pl.ds(pl.multiple_of(b * 256, 256), 256)
    out[0:8, lanes] = real[0:8] - imag[8:16]
    out[8:16, lanes] = imag[0:8] + real[8:16]


def widen(rec, device, field):
    for k in range(4):
        value = rec[device, k // 2, k % 2].astype(F32)
        field[pl.ds(device * 256 + k, 32, stride=8), :] = value
        field[pl.ds(device * 256 + k + 4, 32, stride=8), :] = value


def translate_chunk(base, which_box, which_off, field, table, sums, out, chip):
    for b in range(BOXES):
        total = None
        for j in range(IL):
            row = which_box[base + (j * 4096 + b)]
            operator = which_off[base + (j * 4096 + b)]
            term = field[pl.ds(row, 8), :] * table[pl.ds(operator, 8), :]
            total = term if total is None else total + term
        sums[b * 8 : b * 8 + 8, :] = total
    parts = [sums[pl.ds(k, BOXES, stride=8), :] for k in range(8)]
    out[chip, 0, 0] = (parts[0] - parts[5]).astype(BF16)
    out[chip, 0, 1] = (parts[1] + parts[4]).astype(BF16)
    out[chip, 1, 0] = (parts[2] - parts[7]).astype(BF16)
    out[chip, 1, 1] = (parts[3] + parts[6]).astype(BF16)


def main_kernel(
    cur,
    blocks_in,
    rad_in,
    interp,
    trig,
    oper,
    where,
    box_in,
    off_in,
    rec2,
    near,
    matrix,
    leaf,
    packed,
    rad,
    blocks,
    window,
    ext,
    send,
    rec,
    piece,
    pieces,
    field,
    table,
    sums,
    send2,
    which_box,
    which_off,
    load_sems,
    up_send,
    up_recv,
    pass_send,
    pass_recv,
    down_send,
    down_recv,
    side_send,
    side_recv,
    own_sem,
):
    x, y, z, core = place()
    chip = x * 16 + y * 4 + z
    sibling = (x, (y * 4 + z) * 2 + 1 - core)
    device = chip * 2 + core
    other_at = lax.rem(device + 2 * core - 1 + 128, 128)
    other = (lax.div(other_at, 32), lax.rem(other_at, 32))

    def moved(step, sign):
        tx, ty, tz = [lax.rem(v + 4 + sign * s, 4) for v, s in zip((x, y, z), step)]
        return tx * 16 + ty * 4 + tz, (tx, (ty * 4 + tz) * 2 + core)

    def parted(m):
        return lax.div(m, 16), lax.rem(lax.div(m, 4), 4), lax.rem(m, 4)

    def plane_step(n):
        return lax.rem((n + 1) * 5, 16)

    def up_step(n):
        return parted(plane_step(lax.div(n, 4)) * 4 + lax.rem(lax.rem(n, 4) + 1, 4))

    def down_step(n):
        return parted(lax.rem((n + 1) * 37, CHIPS))

    barrier = pltpu.get_barrier_semaphore()

    def greet(n, carry):
        pl.semaphore_signal(barrier, inc=1, device_id=moved(up_step(n), 1)[1], device_id_type=MESH_ID)
        return carry

    lax.fori_loop(0, CHIPS - 1, greet, 0)
    pl.semaphore_signal(barrier, inc=1, device_id=sibling, device_id_type=MESH_ID)
    pl.semaphore_signal(barrier, inc=1, device_id=other, device_id_type=MESH_ID)

    loads = [
        pltpu.make_async_copy(cur, window.at[1], load_sems.at[0]),
        pltpu.make_async_copy(rad_in, rad, load_sems.at[1]),
        pltpu.make_async_copy(blocks_in, blocks, load_sems.at[2]),
        pltpu.make_async_copy(box_in, which_box, load_sems.at[3]),
        pltpu.make_async_copy(off_in, which_off, load_sems.at[4]),
    ]
    for load in loads:
        load.start()

    build_matrix(interp, trig, matrix)
    piece[...] = jnp.zeros((32, 384), BF16)
    unit = lax.broadcasted_iota(jnp.int32, (16, 16), 0) == lane_ids((16, 16))
    unit = unit.astype(F32).astype(BF16)
    for c in range(2):
        piece[c * 16 : c * 16 + 16, 0:OFFS] = dot_t(unit, oper[c]).astype(BF16)
    loads[0].wait()
    loads[1].wait()
    leaf_patterns(window.at[1], rad, leaf)
    pack_leaves(leaf, packed)

    pl.semaphore_wait(barrier, CHIPS + 1)

    def remote(src, dst, n, to):
        return pltpu.make_async_remote_copy(
            src_ref=src,
            dst_ref=dst,
            send_sem=side_send.at[n],
            recv_sem=side_recv.at[n],
            device_id=to,
            device_id_type=MESH_ID,
        )

    to_sibling = remote(window.at[1], window.at[2 * core], 0, sibling)
    to_other = remote(window.at[1], window.at[2 - 2 * core], 1, other)
    to_sibling.start()
    to_other.start()
    lines = []
    for s in range(3):
        tz = lax.rem(z + s + 1, 4)
        lines.append(remote(piece, pieces.at[z * 2 + core], 2 + s, (x, (y * 4 + tz) * 2 + core)))
        lines[-1].start()
    own_piece = pltpu.make_async_copy(piece, pieces.at[z * 2 + core], load_sems.at[5])
    own_piece.start()

    def up_copy(n):
        to, to_device = moved(up_step(n), 1)
        return pltpu.make_async_remote_copy(
            src_ref=send.at[to],
            dst_ref=rec.at[2 * chip + core],
            send_sem=up_send.at[n],
            recv_sem=up_recv.at[n],
            device_id=to_device,
            device_id_type=MESH_ID,
        )

    def up_block(n, carry):
        plane = plane_step(n)
        kx = lax.rem(x + lax.div(plane, 4), 4)
        ky = lax.rem(y + lax.rem(plane, 4), 4)
        at = kx * 4 + ky
        block = lax.rem(at, 8)
        lanes = pl.ds(pl.multiple_of(block * 256, 256), 256)
        out = dot(packed[lax.div(at, 8)], matrix[:, lanes]).astype(BF16)
        for r in range(R):
            for c in range(2):
                send[at * 4 + r // 2, r % 2, c] = out[r * 32 : r * 32 + 32, c * 128 : c * 128 + 128]
        for s in range(3):
            up_copy(n * 4 + s).start()

        @pl.when(n < 15)
        def _():
            up_copy(n * 4 + 3).start()

        return carry

    lax.fori_loop(0, 16, up_block, 0)
    own = pltpu.make_async_copy(send.at[chip], rec.at[2 * chip + core], own_sem)
    own.start()

    own_piece.wait()
    spread_currents(window, 1, ext)
    ext[3 * NC] = jnp.zeros((16, 128), BF16)
    to_sibling.wait()
    to_other.wait()
    spread_currents(window, 0, ext)
    spread_currents(window, 2, ext)
    loads[2].wait()

    def near_step(b, carry):
        near_box(b, blocks, where, ext, near)
        return carry

    lax.fori_loop(0, BOXES, near_step, 0, unroll=2)

    for line in lines:
        line.wait()
    shares = []
    for s in range(4):
        at = pieces.at[s * 2 + core]
        shares.append(remote(at, at, 5 + s, sibling))
        shares[-1].start()
    own.wait()

    def pass_copy(n, source):
        at = rec.at[2 * source + core]
        return pltpu.make_async_remote_copy(
            src_ref=at,
            dst_ref=at,
            send_sem=pass_send.at[n],
            recv_sem=pass_recv.at[n],
            device_id=sibling,
            device_id_type=MESH_ID,
        )

    pass_copy(CHIPS - 1, chip).start()
    widen(rec, 2 * chip + core, field)

    def arrive(n, carry):
        source = moved(up_step(n), -1)[0]
        up_copy(n).wait_recv()
        pass_copy(n, source).start()
        widen(rec, 2 * source + core, field)
        return carry

    lax.fori_loop(0, CHIPS - 1, arrive, 0)
    for share in shares:
        share.wait()
    for c in range(2):
        rows = [pieces[m, c * 16 : c * 16 + 16, :] for m in range(8)]
        square = jnp.concatenate(rows, axis=0).astype(F32)
        for g in range(3):
            turned = square[:, g * 128 : g * 128 + 128].T
            for k in range(4):
                table[pl.ds(g * 1024 + c * 4 + k, 128, stride=8), :] = turned

    def take(n, carry):
        source = moved(up_step(n), -1)[0]
        at = rec.at[2 * source + 1 - core]
        pltpu.make_async_copy(at, at, pass_recv.at[n]).wait()
        widen(rec, 2 * source + 1 - core, field)
        return carry

    lax.fori_loop(0, CHIPS, take, 0)

    def up_done(n, carry):
        up_copy(n).wait_send()
        pass_copy(n, moved(up_step(n), -1)[0]).wait_send()
        return carry

    lax.fori_loop(0, CHIPS - 1, up_done, 0)
    pass_copy(CHIPS - 1, chip).wait_send()
    loads[3].wait()
    loads[4].wait()

    def down_copy(n):
        to, to_device = moved(down_step(n), 1)
        return pltpu.make_async_remote_copy(
            src_ref=send2.at[to],
            dst_ref=rec2.at[chip],
            send_sem=down_send.at[n],
            recv_sem=down_recv.at[n],
            device_id=to_device,
            device_id_type=MESH_ID,
        )

    def chunk(n, carry):
        to = moved(down_step(n), 1)[0]
        base = to * 64 + core * 32
        translate_chunk(base, which_box, which_off, field, table, sums, send2, to)

        @pl.when(n < CHIPS - 1)
        def _():
            down_copy(n).start()

        return carry

    lax.fori_loop(0, CHIPS, chunk, 0)
    last = pltpu.make_async_copy(send2.at[chip], rec2.at[chip], own_sem)
    last.start()
    last.wait()

    def down_done(n, carry):
        down_copy(n).wait()
        return carry

    lax.fori_loop(0, CHIPS - 1, down_done, 0)


def main_part(cur, blocks, rad, interp, trig, oper, where, which_box, which_off):
    any_spec = pl.BlockSpec(memory_space=pl.ANY)
    sems = pltpu.SemaphoreType.DMA
    return pl.pallas_call(
        main_kernel,
        out_shape=(
            jax.ShapeDtypeStruct((CHIPS, 2, 2, BOXES, 128), BF16),
            jax.ShapeDtypeStruct((16, NC * U), F32),
        ),
        in_specs=[any_spec] * 3 + [VMEM_SPEC] * 3 + [SMEM_SPEC] + [any_spec] * 2,
        out_specs=(VMEM_SPEC, VMEM_SPEC),
        scratch_shapes=[
            pltpu.VMEM((1024, 2048), BF16),
            pltpu.VMEM((16 * 256, 128), F32),
            pltpu.VMEM((2, 256, 1024), BF16),
            pltpu.VMEM((2, NC, U, 128), BF16),
            pltpu.VMEM((2, NC, U, NBR * U), BF16),
            pltpu.VMEM((3, 16, NC * U), BF16),
            pltpu.VMEM((3 * NC + 1, 16, 128), BF16),
            pltpu.VMEM((CHIPS, 2, 2, BOXES, 128), BF16),
            pltpu.VMEM((2 * CHIPS, 2, 2, BOXES, 128), BF16),
            pltpu.VMEM((32, 384), BF16),
            pltpu.VMEM((8, 32, 384), BF16),
            pltpu.VMEM((4096 * 8, 128), F32),
            pltpu.VMEM((384 * 8, 128), F32),
            pltpu.VMEM((BOXES * 8, 128), F32),
            pltpu.VMEM((CHIPS, 2, 2, BOXES, 128), BF16),
            pltpu.SMEM((4096 * IL,), jnp.int32),
            pltpu.SMEM((4096 * IL,), jnp.int32),
            sems((6,)),
            sems((CHIPS,)),
            sems((CHIPS,)),
            sems((CHIPS,)),
            sems((CHIPS,)),
            sems((CHIPS,)),
            sems((CHIPS,)),
            sems((9,)),
            sems((9,)),
            sems,
        ],
        compiler_params=pltpu.CompilerParams(
            collective_id=1, has_side_effects=True, vmem_limit_bytes=60 << 20
        ),
        name="up_near_translate",
    )(cur, blocks, rad, interp, trig, oper, where, which_box, which_off)


def down_kernel(rec, rad, interp, trig, near, out, matrix, leaf):
    build_matrix(interp, trig, matrix)
    left = lane_ids((256, 128)) < 64
    for c in range(2):
        for half in range(2):
            rows = slice(c * 512 + half * 256, c * 512 + half * 256 + 256)
            results = []
            for p in range(2):
                pieces = []
                for block in range(8):
                    for c2 in range(2):
                        at = (p * 8 + block) * 8
                        pieces.append(rec[at : at + 8, c2].reshape(256, 128))
                fields = jnp.concatenate(pieces, axis=1)
                results.append(dot_t(fields, matrix[rows, :]))
            for m in range(2):
                first = results[0][:, m * 128 : m * 128 + 128]
                second = results[1][:, m * 128 : m * 128 + 128]
                at = (c * 8 + half * 4 + m * 2) * 256
                leaf[at : at + 256, :] = jnp.where(left, first, pltpu.roll(second, 64, 1))
                leaf[at + 256 : at + 512, :] = jnp.where(left, pltpu.roll(first, 64, 1), second)
    own = lane_ids((16, 256)) // U

    def box(b, carry):
        pieces = []
        for i in range(8):
            for c in range(2):
                pieces.append(leaf[pl.ds((c * 8 + i) * 256 + b, 8, stride=32), :])
        stacked = jnp.concatenate(pieces, axis=0).astype(BF16)
        sums = []
        for c in range(2):
            result = dot_t(stacked, rad[c, pl.ds(b * 8, 8)].reshape(256, 128))
            total = jnp.zeros((16, 256), F32)
            for i in range(8):
                total = jnp.where(own == i, result[i * 16 : i * 16 + 16], total)
            sums.append(total)
        real, imag = sums
        lanes = pl.ds(pl.multiple_of(b * 256, 256), 256)
        out[0:8, lanes] = near[0:8, lanes] + (real[0:8] + imag[8:16])
        out[8:16, lanes] = near[8:16, lanes] + (real[8:16] - imag[0:8])
        return carry

    lax.fori_loop(0, BOXES, box, 0, unroll=2)


def downward(rec, rad, interp, trig, near):
    return pl.pallas_call(
        down_kernel,
        out_shape=jax.ShapeDtypeStruct((16, NC * U), F32),
        in_specs=[VMEM_SPEC] * 5,
        out_specs=VMEM_SPEC,
        scratch_shapes=[
            pltpu.VMEM((1024, 2048), BF16),
            pltpu.VMEM((16 * 256, 128), F32),
        ],
        compiler_params=pltpu.CompilerParams(vmem_limit_bytes=40 << 20),
        name="downward",
    )(rec, rad, interp, trig, near)


def local(
    currents,
    near_blocks,
    near_list,
    near_count,
    radiation,
    interp,
    shift_angle,
    translation,
    trans_box,
    trans_off,
):
    device = lax.axis_index(AXES)
    cur = currents.reshape(16, NC * U)
    slots = jnp.arange(NBR, dtype=jnp.int32)
    row = near_list.T - (device * NC - NC)
    where = jnp.where(slots[:, None] < near_count[None, :], row, 3 * NC)
    where = where.reshape(NC * NBR)
    which_box = (trans_box.T * 8).reshape(4096 * IL)
    which_off = (trans_off.T * 8).reshape(4096 * IL)
    trig = jnp.concatenate([jnp.cos(shift_angle), jnp.sin(shift_angle)], axis=0)
    received, near = main_part(
        cur, near_blocks, radiation, interp, trig, translation, where, which_box, which_off
    )
    out = downward(received.reshape(128, 2, BOXES, 128), radiation, interp, trig, near)
    return out.reshape(2, R, NC * U)


def solution(mesh):
    placed = (
        P(None, None, AXES),
        P(None, AXES, None, None),
        P(AXES, None),
        P(AXES),
        P(None, AXES, None, None),
        P(),
        P(),
        P(None, None, AXES),
        P(),
        P(),
    )
    return jax.shard_map(
        local, mesh=mesh, in_specs=placed, out_specs=P(None, None, AXES), check_vma=False
    )
```

time: 169 us -> 122 us (0.72); the launches traced: 169 us -> 120 us
  Pallas kernels: 135 us -> 107 us
  blocking collectives: 14.2 us -> 0 us
  starting transfers between devices: 6.85 us -> 0 us
  other arithmetic: 0.24 us -> 3.28 us
  local copies, waits for them, and re-layouts: 12.1 us -> 9.32 us
    pallas_call x5 -> x1, Pallas kernels: 127 us -> 99.6 us  [main_part(): pl.pallas_call(main_kernel, out_shape=(jax.ShapeDtypeStruct((CHIPS, 2, 2,...]
    all_gather x1 -> x0, blocking collectives: 14.2 us -> none  [local(): lax.all_gather(translation, 'smp', axis_index_groups=groups, axis=2, tile...]
    ppermute x2 -> x0, starting transfers between devices: 6.85 us -> none  [passed_along(): return lax.ppermute(array, AXES, pairs)]
    reshape x3 -> x2, local copies, waits for them, and re-layouts: 3.93 us -> 1.47 us  [the longest x1 0.74 us: local(): which_off = (trans_off.T * 8).reshape(4096 * IL)]
    mul x2, other arithmetic: 0.21 us -> 1.94 us  [the longest x1 0.97 us: local(): which_box = (trans_box.T * 8).reshape(4096 * IL)]
    unnamed x23 -> x12, local copies, waits for them, and re-layouts: 7.87 us -> 6.96 us
  transfers between devices with their start and end apart: 2 -> 0, of which waited for: 0 -> 0; matrix products, arithmetic and copies ran while one was open for 4% -> 0% of each run, Pallas kernels for 71% -> 0%
where the time goes in v2:
time: 122 us; the launch traced here: 120 us
  Pallas kernels  107 us (88%)
  local copies, waits for them, and re-layouts  9.32 us (8%)
  other arithmetic  3.28 us (3%)
    pallas_call x1, Pallas kernels, main_part(): pl.pallas_call(main_kernel, out_shape=(jax.ShapeDtypeStruct((CHIPS, 2, 2,...  99.6 us
    pallas_call x1, Pallas kernels, downward(): pl.pallas_call(down_kernel, out_shape=jax.ShapeDtypeStruct((16, NC * U),...  7.73 us
    unnamed x12, local copies, waits for them, and re-layouts  6.96 us

profile of v2, /device:TPU:1, one launch (start us, length us, event | category | flops | bytes accessed | tf_op | source)
XLA Modules:
  0.0 120.0 jit_solution(10390381216110864298)
XLA Ops:
  0.0 0.7 fusion
  0.7 0.6 copy.12
  1.3 0.9 fusion.1
  2.2 0.6 pad_maximum_fusion.trig
  2.8 1.5 %copy.11.oper = bf16[2,316,16]{2,1,0:T(8,128)(2,1)} copy(bf16[2,316,16]{1,2,0:T(8,128)(2,1)} %param.17) | data formatting | bytes 40448 | tf_op args[7]
  4.4 1.0 multiply_bitcast_fusion.1
  5.3 0.7 reshape.21.box_in
  6.1 1.0 multiply_bitcast_fusion
  7.0 0.7 reshape.22.off_in
  7.8 0.0 copy-start.2
  7.8 0.0 copy-start.3
  7.8 99.6 %up_near_translate.1 = (bf16[64,2,2,32,128]{4,3,2,1,0:T(8,128)(2,1)}, f32[16,8192]{1,0:T(8,128)}) custom-call(bf16[16,8192]{1,0:T(8,128)(2,1)} %bitcast.15, bf16[2,256,32,256]{3,2,1,0:T(8,128)(2,1)} %blocks_in.1, bf16[2,256,32,128]{3,2,1,0:T(8,128)(2,1)} %rad.1, bf16[64,1024]{1,0:T(8,128)(2,1)} %interp.3, f32[16,1024]{1,0:T(8,128)} %pad_maximum_fusion.trig, ...), custom_call_target="tpu_custom_call" | custom-call | tf_op jit(solution)/shard_map/up_near_translate/pallas_call | solution.py:429
  107.4 0.0 copy-done.2
  107.4 0.0 copy-done.3
  107.4 0.0 copy-start
  107.5 2.2 %copy-done = bf16[2,256,32,128]{3,2,1,0:T(8,128)(2,1)S(1)} copy-done((bf16[2,256,32,128]{3,2,1,0:T(8,128)(2,1)S(1)}, bf16[2,256,32,128]{3,2,1,0:T(8,128)(2,1)}, u32[]{:S(2)}) %copy-start) | copy-done | bytes 4194328
  109.6 0.0 copy-start.1
  109.6 1.6 %copy-done.1 = bf16[64,2,2,32,128]{4,3,2,1,0:T(8,128)(2,1)S(1)} copy-done((bf16[64,2,2,32,128]{4,3,2,1,0:T(8,128)(2,1)S(1)}, bf16[64,2,2,32,128]{4,3,2,1,0:T(8,128)(2,1)}, u32[]{:S(2)}) %copy-start.1) | copy-done | bytes 2097176
  111.2 0.0 copy-start.4
  111.2 1.0 copy-done.4
  112.3 7.7 %downward.1 = f32[16,8192]{1,0:T(8,128)} custom-call(bf16[128,2,32,128]{3,2,1,0:T(8,128)(2,1)S(1)} %bitcast.14, bf16[2,256,32,128]{3,2,1,0:T(8,128)(2,1)S(1)} %copy-done, bf16[64,1024]{1,0:T(8,128)(2,1)S(1)} %copy-done.3, f32[16,1024]{1,0:T(8,128)S(1)} %copy-done.2, f32[16,8192]{1,0:T(8,128)S(1)} %copy-done.4), custom_call_target="tpu_custom_call" | custom-call | tf_op jit(solution)/shard_map/downward/pallas_call | solution.py:519
Async XLA Ops:
  7.8 99.6 %copy-start.2 = (f32[16,1024]{1,0:T(8,128)S(1)}, f32[16,1024]{1,0:T(8,128)}, u32[]{:S(2)}) copy-start(f32[16,1024]{1,0:T(8,128)} %pad_maximum_fusion.trig) | copy-start | bytes 196612
  7.8 99.6 %copy-start.3 = (bf16[64,1024]{1,0:T(8,128)(2,1)S(1)}, bf16[64,1024]{1,0:T(8,128)(2,1)}, u32[]{:S(2)}) copy-start(bf16[64,1024]{1,0:T(8,128)(2,1)} %interp.3) | copy-start | bytes 393220
  107.4 2.2 %copy-start = (bf16[2,256,32,128]{3,2,1,0:T(8,128)(2,1)S(1)}, bf16[2,256,32,128]{3,2,1,0:T(8,128)(2,1)}, u32[]{:S(2)}) copy-start(bf16[2,256,32,128]{3,2,1,0:T(8,128)(2,1)} %rad.1) | copy-start | bytes 12582916
  109.6 1.6 %copy-start.1 = (bf16[64,2,2,32,128]{4,3,2,1,0:T(8,128)(2,1)S(1)}, bf16[64,2,2,32,128]{4,3,2,1,0:T(8,128)(2,1)}, u32[]{:S(2)}) copy-start(bf16[64,2,2,32,128]{4,3,2,1,0:T(8,128)(2,1)} %get-tuple-element.7) | copy-start | bytes 6291460
  111.2 1.0 copy-start.4

commit v3 on v2

--- a/solution.py
+++ b/solution.py
@@ -44,7 +44,9 @@
     return lax.broadcasted_iota(jnp.int32, shape, 1)
 
 
-def build_matrix(interp, trig, matrix):
+def build_matrix(interp, angle, matrix, trig):
+    trig[0:8, :] = jnp.cos(angle[...])
+    trig[8:16, :] = jnp.sin(angle[...])
     for block in range(8):
         lanes = slice(block * 128, block * 128 + 128)
         table = interp[:, lanes].astype(F32)
@@ -161,19 +163,67 @@
     out[chip, 1, 1] = (parts[3] + parts[6]).astype(BF16)
 
 
+def unpack_fields(rec2, matrix, leaf):
+    left = lane_ids((256, 128)) < 64
+    for c in range(2):
+        for half in range(2):
+            rows = slice(c * 512 + half * 256, c * 512 + half * 256 + 256)
+            results = []
+            for p in range(2):
+                pieces = []
+                for block in range(8):
+                    for c2 in range(2):
+                        at = (p * 8 + block) * 4
+                        pieces.append(rec2[at : at + 4, :, c2].reshape(256, 128))
+                fields = jnp.concatenate(pieces, axis=1)
+                results.append(dot_t(fields, matrix[rows, :]))
+            for m in range(2):
+                first = results[0][:, m * 128 : m * 128 + 128]
+                second = results[1][:, m * 128 : m * 128 + 128]
+                at = (c * 8 + half * 4 + m * 2) * 256
+                leaf[at : at + 256, :] = jnp.where(left, first, pltpu.roll(second, 64, 1))
+                leaf[at + 256 : at + 512, :] = jnp.where(left, pltpu.roll(first, 64, 1), second)
+
+
+def far_boxes(leaf, rad, out):
+    own = lane_ids((16, 256)) // U
+
+    def box(b, carry):
+        pieces = []
+        for i in range(8):
+            for c in range(2):
+                pieces.append(leaf[pl.ds((c * 8 + i) * 256 + b, 8, stride=32), :])
+        stacked = jnp.concatenate(pieces, axis=0).astype(BF16)
+        sums = []
+        for c in range(2):
+            result = dot_t(stacked, rad[c, pl.ds(b * 8, 8)].reshape(256, 128))
+            total = jnp.zeros((16, 256), F32)
+            for i in range(8):
+                total = jnp.where(own == i, result[i * 16 : i * 16 + 16], total)
+            sums.append(total)
+        real, imag = sums
+        lanes = pl.ds(pl.multiple_of(b * 256, 256), 256)
+        out[0:8, lanes] += real[0:8] + imag[8:16]
+        out[8:16, lanes] += real[8:16] - imag[0:8]
+        return carry
+
+    lax.fori_loop(0, BOXES, box, 0, unroll=2)
+
+
 def main_kernel(
     cur,
     blocks_in,
     rad_in,
     interp,
-    trig,
+    angle,
     oper,
-    where,
+    list_in,
+    count_in,
     box_in,
     off_in,
-    rec2,
-    near,
+    out,
     matrix,
+    trig,
     leaf,
     packed,
     rad,
@@ -188,9 +238,17 @@
     table,
     sums,
     send2,
+    rec2,
+    rows_here,
+    boxes_here,
+    offs_here,
+    where,
     which_box,
     which_off,
     load_sems,
+    list_sems,
+    box_sems,
+    off_sems,
     up_send,
     up_recv,
     pass_send,
@@ -208,52 +266,59 @@
     other_at = lax.rem(device + 2 * core - 1 + 128, 128)
     other = (lax.div(other_at, 32), lax.rem(other_at, 32))
 
-    def moved(step, sign):
+    def moved(n, sign):
+        m = lax.rem((n + 1) * 37, CHIPS)
+        step = (lax.div(m, 16), lax.rem(lax.div(m, 4), 4), lax.rem(m, 4))
         tx, ty, tz = [lax.rem(v + 4 + sign * s, 4) for v, s in zip((x, y, z), step)]
         return tx * 16 + ty * 4 + tz, (tx, (ty * 4 + tz) * 2 + core)
-
-    def parted(m):
-        return lax.div(m, 16), lax.rem(lax.div(m, 4), 4), lax.rem(m, 4)
-
-    def plane_step(n):
-        return lax.rem((n + 1) * 5, 16)
-
-    def up_step(n):
-        return parted(plane_step(lax.div(n, 4)) * 4 + lax.rem(lax.rem(n, 4) + 1, 4))
-
-    def down_step(n):
-        return parted(lax.rem((n + 1) * 37, CHIPS))
-
-    barrier = pltpu.get_barrier_semaphore()
-
-    def greet(n, carry):
-        pl.semaphore_signal(barrier, inc=1, device_id=moved(up_step(n), 1)[1], device_id_type=MESH_ID)
-        return carry
-
-    lax.fori_loop(0, CHIPS - 1, greet, 0)
-    pl.semaphore_signal(barrier, inc=1, device_id=sibling, device_id_type=MESH_ID)
-    pl.semaphore_signal(barrier, inc=1, device_id=other, device_id_type=MESH_ID)
 
     loads = [
         pltpu.make_async_copy(cur, window.at[1], load_sems.at[0]),
         pltpu.make_async_copy(rad_in, rad, load_sems.at[1]),
         pltpu.make_async_copy(blocks_in, blocks, load_sems.at[2]),
-        pltpu.make_async_copy(box_in, which_box, load_sems.at[3]),
-        pltpu.make_async_copy(off_in, which_off, load_sems.at[4]),
     ]
     for load in loads:
         load.start()
-
-    build_matrix(interp, trig, matrix)
+    barrier = pltpu.get_barrier_semaphore()
+
+    def greet(n, carry):
+        pl.semaphore_signal(barrier, inc=1, device_id=moved(n, 1)[1], device_id_type=MESH_ID)
+        return carry
+
+    lax.fori_loop(0, CHIPS - 1, greet, 0)
+    pl.semaphore_signal(barrier, inc=1, device_id=sibling, device_id_type=MESH_ID)
+    pl.semaphore_signal(barrier, inc=1, device_id=other, device_id_type=MESH_ID)
+
+    slots = lax.broadcasted_iota(jnp.int32, (NBR, NC), 0)
+    rows_here[...] = jnp.where(slots < count_in[...], list_in[...] - (device * NC - NC), 3 * NC)
+    boxes_here[...] = box_in[...] * 8
+    offs_here[...] = off_in[...] * 8
+    lists = []
+    for k in range(NBR):
+        lists.append(
+            pltpu.make_async_copy(rows_here.at[k], where.at[pl.ds(k * NC, NC)], list_sems.at[k])
+        )
+    for j in range(IL):
+        part = pl.ds(j * 4096, 4096)
+        lists.append(pltpu.make_async_copy(boxes_here.at[j], which_box.at[part], box_sems.at[j]))
+        lists.append(pltpu.make_async_copy(offs_here.at[j], which_off.at[part], off_sems.at[j]))
+    for copy in lists:
+        copy.start()
+
+    build_matrix(interp, angle, matrix, trig)
     piece[...] = jnp.zeros((32, 384), BF16)
-    unit = lax.broadcasted_iota(jnp.int32, (16, 16), 0) == lane_ids((16, 16))
-    unit = unit.astype(F32).astype(BF16)
     for c in range(2):
-        piece[c * 16 : c * 16 + 16, 0:OFFS] = dot_t(unit, oper[c]).astype(BF16)
+        piece[c * 16 : c * 16 + 16, 0:OFFS] = oper[c]
     loads[0].wait()
     loads[1].wait()
     leaf_patterns(window.at[1], rad, leaf)
     pack_leaves(leaf, packed)
+    for at in range(16):
+        lanes = slice(at % 8 * 256, at % 8 * 256 + 256)
+        result = dot(packed[at // 8], matrix[:, lanes]).astype(BF16)
+        for r in range(R):
+            for c in range(2):
+                send[at * 4 + r // 2, r % 2, c] = result[r * 32 : r * 32 + 32, c * 128 : c * 128 + 128]
 
     pl.semaphore_wait(barrier, CHIPS + 1)
 
@@ -276,11 +341,9 @@
         tz = lax.rem(z + s + 1, 4)
         lines.append(remote(piece, pieces.at[z * 2 + core], 2 + s, (x, (y * 4 + tz) * 2 + core)))
         lines[-1].start()
-    own_piece = pltpu.make_async_copy(piece, pieces.at[z * 2 + core], load_sems.at[5])
-    own_piece.start()
 
     def up_copy(n):
-        to, to_device = moved(up_step(n), 1)
+        to, to_device = moved(n, 1)
         return pltpu.make_async_remote_copy(
             src_ref=send.at[to],
             dst_ref=rec.at[2 * chip + core],
@@ -290,45 +353,17 @@
             device_id_type=MESH_ID,
         )
 
-    def up_block(n, carry):
-        plane = plane_step(n)
-        kx = lax.rem(x + lax.div(plane, 4), 4)
-        ky = lax.rem(y + lax.rem(plane, 4), 4)
-        at = kx * 4 + ky
-        block = lax.rem(at, 8)
-        lanes = pl.ds(pl.multiple_of(block * 256, 256), 256)
-        out = dot(packed[lax.div(at, 8)], matrix[:, lanes]).astype(BF16)
-        for r in range(R):
-            for c in range(2):
-                send[at * 4 + r // 2, r % 2, c] = out[r * 32 : r * 32 + 32, c * 128 : c * 128 + 128]
-        for s in range(3):
-            up_copy(n * 4 + s).start()
-
-        @pl.when(n < 15)
-        def _():
-            up_copy(n * 4 + 3).start()
-
-        return carry
-
-    lax.fori_loop(0, 16, up_block, 0)
+    def up_start(n, carry):
+        up_copy(n).start()
+        return carry
+
+    lax.fori_loop(0, CHIPS - 1, up_start, 0)
+    own_piece = pltpu.make_async_copy(piece, pieces.at[z * 2 + core], load_sems.at[3])
+    own_piece.start()
     own = pltpu.make_async_copy(send.at[chip], rec.at[2 * chip + core], own_sem)
     own.start()
 
     own_piece.wait()
-    spread_currents(window, 1, ext)
-    ext[3 * NC] = jnp.zeros((16, 128), BF16)
-    to_sibling.wait()
-    to_other.wait()
-    spread_currents(window, 0, ext)
-    spread_currents(window, 2, ext)
-    loads[2].wait()
-
-    def near_step(b, carry):
-        near_box(b, blocks, where, ext, near)
-        return carry
-
-    lax.fori_loop(0, BOXES, near_step, 0, unroll=2)
-
     for line in lines:
         line.wait()
     shares = []
@@ -338,8 +373,8 @@
         shares[-1].start()
     own.wait()
 
-    def pass_copy(n, source):
-        at = rec.at[2 * source + core]
+    def pass_copy(n):
+        at = rec.at[2 * moved(n, -1)[0] + core]
         return pltpu.make_async_remote_copy(
             src_ref=at,
             dst_ref=at,
@@ -349,17 +384,14 @@
             device_id_type=MESH_ID,
         )
 
-    pass_copy(CHIPS - 1, chip).start()
+    pass_copy(CHIPS - 1).start()
     widen(rec, 2 * chip + core, field)
-
-    def arrive(n, carry):
-        source = moved(up_step(n), -1)[0]
-        up_copy(n).wait_recv()
-        pass_copy(n, source).start()
-        widen(rec, 2 * source + core, field)
-        return carry
-
-    lax.fori_loop(0, CHIPS - 1, arrive, 0)
+    spread_currents(window, 1, ext)
+    ext[3 * NC] = jnp.zeros((16, 128), BF16)
+    to_sibling.wait()
+    to_other.wait()
+    spread_currents(window, 0, ext)
+    spread_currents(window, 2, ext)
     for share in shares:
         share.wait()
     for c in range(2):
@@ -369,28 +401,42 @@
             turned = square[:, g * 128 : g * 128 + 128].T
             for k in range(4):
                 table[pl.ds(g * 1024 + c * 4 + k, 128, stride=8), :] = turned
-
-    def take(n, carry):
-        source = moved(up_step(n), -1)[0]
+    loads[2].wait()
+    for copy in lists:
+        copy.wait()
+
+    def arrive(n):
+        up_copy(n).wait_recv()
+        pass_copy(n).start()
+        widen(rec, 2 * moved(n, -1)[0] + core, field)
+
+    def take(n):
+        source = moved(n, -1)[0]
         at = rec.at[2 * source + 1 - core]
         pltpu.make_async_copy(at, at, pass_recv.at[n]).wait()
         widen(rec, 2 * source + 1 - core, field)
-        return carry
-
-    lax.fori_loop(0, CHIPS, take, 0)
-
-    def up_done(n, carry):
-        up_copy(n).wait_send()
-        pass_copy(n, moved(up_step(n), -1)[0]).wait_send()
-        return carry
-
-    lax.fori_loop(0, CHIPS - 1, up_done, 0)
-    pass_copy(CHIPS - 1, chip).wait_send()
-    loads[3].wait()
-    loads[4].wait()
+
+    def near_step(b, carry):
+        near_box(b, blocks, where, ext, out)
+        arrive(2 * b)
+
+        @pl.when(b < 31)
+        def _():
+            arrive(2 * b + 1)
+
+        @pl.when(b >= 2)
+        def _():
+            take(2 * b - 4)
+            take(2 * b - 3)
+
+        return carry
+
+    lax.fori_loop(0, BOXES, near_step, 0)
+    for n in range(CHIPS - 4, CHIPS):
+        take(n)
 
     def down_copy(n):
-        to, to_device = moved(down_step(n), 1)
+        to, to_device = moved(n, 1)
         return pltpu.make_async_remote_copy(
             src_ref=send2.at[to],
             dst_ref=rec2.at[chip],
@@ -401,7 +447,7 @@
         )
 
     def chunk(n, carry):
-        to = moved(down_step(n), 1)[0]
+        to = moved(n, 1)[0]
         base = to * 64 + core * 32
         translate_chunk(base, which_box, which_off, field, table, sums, send2, to)
 
@@ -414,6 +460,14 @@
     lax.fori_loop(0, CHIPS, chunk, 0)
     last = pltpu.make_async_copy(send2.at[chip], rec2.at[chip], own_sem)
     last.start()
+
+    def up_done(n, carry):
+        up_copy(n).wait_send()
+        pass_copy(n).wait_send()
+        return carry
+
+    lax.fori_loop(0, CHIPS - 1, up_done, 0)
+    pass_copy(CHIPS - 1).wait_send()
     last.wait()
 
     def down_done(n, carry):
@@ -421,21 +475,21 @@
         return carry
 
     lax.fori_loop(0, CHIPS - 1, down_done, 0)
-
-
-def main_part(cur, blocks, rad, interp, trig, oper, where, which_box, which_off):
+    unpack_fields(rec2, matrix, leaf)
+    far_boxes(leaf, rad, out)
+
+
+def main_part(cur, blocks, rad, interp, angle, oper, near_rows, near_count, box, off):
     any_spec = pl.BlockSpec(memory_space=pl.ANY)
     sems = pltpu.SemaphoreType.DMA
     return pl.pallas_call(
         main_kernel,
-        out_shape=(
-            jax.ShapeDtypeStruct((CHIPS, 2, 2, BOXES, 128), BF16),
-            jax.ShapeDtypeStruct((16, NC * U), F32),
-        ),
-        in_specs=[any_spec] * 3 + [VMEM_SPEC] * 3 + [SMEM_SPEC] + [any_spec] * 2,
-        out_specs=(VMEM_SPEC, VMEM_SPEC),
+        out_shape=jax.ShapeDtypeStruct((16, NC * U), F32),
+        in_specs=[any_spec] * 3 + [VMEM_SPEC] * 7,
+        out_specs=VMEM_SPEC,
         scratch_shapes=[
             pltpu.VMEM((1024, 2048), BF16),
+            pltpu.VMEM((16, 1024), F32),
             pltpu.VMEM((16 * 256, 128), F32),
             pltpu.VMEM((2, 256, 1024), BF16),
             pltpu.VMEM((2, NC, U, 128), BF16),
@@ -450,9 +504,17 @@
             pltpu.VMEM((384 * 8, 128), F32),
             pltpu.VMEM((BOXES * 8, 128), F32),
             pltpu.VMEM((CHIPS, 2, 2, BOXES, 128), BF16),
+            pltpu.VMEM((CHIPS, 2, 2, BOXES, 128), BF16),
+            pltpu.VMEM((NBR, NC), jnp.int32),
+            pltpu.VMEM((IL, 4096), jnp.int32),
+            pltpu.VMEM((IL, 4096), jnp.int32),
+            pltpu.SMEM((NC * NBR,), jnp.int32),
             pltpu.SMEM((4096 * IL,), jnp.int32),
             pltpu.SMEM((4096 * IL,), jnp.int32),
-            sems((6,)),
+            sems((4,)),
+            sems((NBR,)),
+            sems((IL,)),
+            sems((IL,)),
             sems((CHIPS,)),
             sems((CHIPS,)),
             sems((CHIPS,)),
@@ -467,67 +529,7 @@
             collective_id=1, has_side_effects=True, vmem_limit_bytes=60 << 20
         ),
         name="up_near_translate",
-    )(cur, blocks, rad, interp, trig, oper, where, which_box, which_off)
-
-
-def down_kernel(rec, rad, interp, trig, near, out, matrix, leaf):
-    build_matrix(interp, trig, matrix)
-    left = lane_ids((256, 128)) < 64
-    for c in range(2):
-        for half in range(2):
-            rows = slice(c * 512 + half * 256, c * 512 + half * 256 + 256)
-            results = []
-            for p in range(2):
-                pieces = []
-                for block in range(8):
-                    for c2 in range(2):
-                        at = (p * 8 + block) * 8
-                        pieces.append(rec[at : at + 8, c2].reshape(256, 128))
-                fields = jnp.concatenate(pieces, axis=1)
-                results.append(dot_t(fields, matrix[rows, :]))
-            for m in range(2):
-                first = results[0][:, m * 128 : m * 128 + 128]
-                second = results[1][:, m * 128 : m * 128 + 128]
-                at = (c * 8 + half * 4 + m * 2) * 256
-                leaf[at : at + 256, :] = jnp.where(left, first, pltpu.roll(second, 64, 1))
-                leaf[at + 256 : at + 512, :] = jnp.where(left, pltpu.roll(first, 64, 1), second)
-    own = lane_ids((16, 256)) // U
-
-    def box(b, carry):
-        pieces = []
-        for i in range(8):
-            for c in range(2):
-                pieces.append(leaf[pl.ds((c * 8 + i) * 256 + b, 8, stride=32), :])
-        stacked = jnp.concatenate(pieces, axis=0).astype(BF16)
-        sums = []
-        for c in range(2):
-            result = dot_t(stacked, rad[c, pl.ds(b * 8, 8)].reshape(256, 128))
-            total = jnp.zeros((16, 256), F32)
-            for i in range(8):
-                total = jnp.where(own == i, result[i * 16 : i * 16 + 16], total)
-            sums.append(total)
-        real, imag = sums
-        lanes = pl.ds(pl.multiple_of(b * 256, 256), 256)
-        out[0:8, lanes] = near[0:8, lanes] + (real[0:8] + imag[8:16])
-        out[8:16, lanes] = near[8:16, lanes] + (real[8:16] - imag[0:8])
-        return carry
-
-    lax.fori_loop(0, BOXES, box, 0, unroll=2)
-
-
-def downward(rec, rad, interp, trig, near):
-    return pl.pallas_call(
-        down_kernel,
-        out_shape=jax.ShapeDtypeStruct((16, NC * U), F32),
-        in_specs=[VMEM_SPEC] * 5,
-        out_specs=VMEM_SPEC,
-        scratch_shapes=[
-            pltpu.VMEM((1024, 2048), BF16),
-            pltpu.VMEM((16 * 256, 128), F32),
-        ],
-        compiler_params=pltpu.CompilerParams(vmem_limit_bytes=40 << 20),
-        name="downward",
-    )(rec, rad, interp, trig, near)
+    )(cur, blocks, rad, interp, angle, oper, near_rows, near_count, box, off)
 
 
 def local(
@@ -542,19 +544,18 @@
     trans_box,
     trans_off,
 ):
-    device = lax.axis_index(AXES)
-    cur = currents.reshape(16, NC * U)
-    slots = jnp.arange(NBR, dtype=jnp.int32)
-    row = near_list.T - (device * NC - NC)
-    where = jnp.where(slots[:, None] < near_count[None, :], row, 3 * NC)
-    where = where.reshape(NC * NBR)
-    which_box = (trans_box.T * 8).reshape(4096 * IL)
-    which_off = (trans_off.T * 8).reshape(4096 * IL)
-    trig = jnp.concatenate([jnp.cos(shift_angle), jnp.sin(shift_angle)], axis=0)
-    received, near = main_part(
-        cur, near_blocks, radiation, interp, trig, translation, where, which_box, which_off
+    out = main_part(
+        currents.reshape(16, NC * U),
+        near_blocks,
+        radiation,
+        interp,
+        shift_angle,
+        translation.transpose(0, 2, 1),
+        near_list.T,
+        near_count.reshape(1, NC),
+        trans_box.T,
+        trans_off.T,
     )
-    out = downward(received.reshape(128, 2, BOXES, 128), radiation, interp, trig, near)
     return out.reshape(2, R, NC * U)
 
 

time: 122 us -> 114 us (0.934); the launches traced: 120 us -> 114 us
  local copies, waits for them, and re-layouts: 9.32 us -> 1.87 us
  Pallas kernels: 107 us -> 112 us
  other arithmetic: 3.28 us -> 0 us
    unnamed x12 -> x1, local copies, waits for them, and re-layouts: 6.96 us -> 1.87 us
    pallas_call x2 -> x1, Pallas kernels: 107 us -> 112 us  [main_part(): pl.pallas_call(main_kernel, out_shape=jax.ShapeDtypeStruct((16, NC * U),...]
    mul x2 -> x0, other arithmetic: 1.94 us -> none  [the longest x1 0.97 us: local(): which_box = (trans_box.T * 8).reshape(4096 * IL)]
    reshape x2 -> x0, local copies, waits for them, and re-layouts: 1.47 us -> none  [the longest x1 0.74 us: local(): which_off = (trans_off.T * 8).reshape(4096 * IL)]
where the time goes in v3:
time: 114 us
  Pallas kernels  112 us (98%)
  local copies, waits for them, and re-layouts  1.87 us (2%)
    pallas_call x1, Pallas kernels, main_part(): pl.pallas_call(main_kernel, out_shape=jax.ShapeDtypeStruct((16, NC * U),...  112 us

profile of v3, /device:TPU:1, one launch (start us, length us, event | category | flops | bytes accessed | tf_op | source)
XLA Modules:
  0.0 114.1 jit_solution(9631312769526749560)
XLA Ops:
  0.0 112.2 %up_near_translate.1 = f32[16,8192]{1,0:T(8,128)} custom-call(bf16[16,8192]{1,0:T(8,128)(2,1)} %bitcast.8, bf16[2,256,32,256]{3,2,1,0:T(8,128)(2,1)} %blocks_in.1, bf16[2,256,32,128]{3,2,1,0:T(8,128)(2,1)} %rad_in.1, bf16[64,1024]{1,0:T(8,128)(2,1)} %interp.1, f32[8,1024]{1,0:T(8,128)} %angle.1, bf16[2,16,316]{2,1,0:T(8,128)(2,1)} %bitcast.11, ...), custom_call_target="tpu_custom_call" | custom-call | tf_op jit(solution)/shard_map/up_near_translate/pallas_call | solution.py:485
  112.2 1.9 %copy.12 = f32[2,8,8192]{2,1,0:T(8,128)} copy(f32[2,8,8192]{2,1,0:T(8,128)} %bitcast.7) | data formatting | bytes 1048576

commit v4 on v3

--- a/solution.py
+++ b/solution.py
@@ -14,6 +14,8 @@
 NC = 256
 OFFS = 316
 BOXES = 32
+WINDOW = 32
+GROUP = 4
 CHIPS = 64
 AXES = ("grp", "smp")
 MESH_ID = pl.DeviceIdType.MESH
@@ -140,19 +142,20 @@
     out[8:16, lanes] = imag[0:8] + real[8:16]
 
 
-def widen(rec, device, field):
+def widen(rec, half, n, device, field):
     for k in range(4):
-        value = rec[device, k // 2, k % 2].astype(F32)
+        value = rec[half, n, k // 2, k % 2].astype(F32)
         field[pl.ds(device * 256 + k, 32, stride=8), :] = value
         field[pl.ds(device * 256 + k + 4, 32, stride=8), :] = value
 
 
 def translate_chunk(base, which_box, which_off, field, table, sums, out, chip):
+    starts = [base + j * 4096 for j in range(IL)]
     for b in range(BOXES):
         total = None
         for j in range(IL):
-            row = which_box[base + (j * 4096 + b)]
-            operator = which_off[base + (j * 4096 + b)]
+            row = which_box[starts[j] + b]
+            operator = which_off[starts[j] + b]
             term = field[pl.ds(row, 8), :] * table[pl.ds(operator, 8), :]
             total = term if total is None else total + term
         sums[b * 8 : b * 8 + 8, :] = total
@@ -277,8 +280,8 @@
         pltpu.make_async_copy(rad_in, rad, load_sems.at[1]),
         pltpu.make_async_copy(blocks_in, blocks, load_sems.at[2]),
     ]
-    for load in loads:
-        load.start()
+    loads[0].start()
+    loads[1].start()
     barrier = pltpu.get_barrier_semaphore()
 
     def greet(n, carry):
@@ -289,28 +292,25 @@
     pl.semaphore_signal(barrier, inc=1, device_id=sibling, device_id_type=MESH_ID)
     pl.semaphore_signal(barrier, inc=1, device_id=other, device_id_type=MESH_ID)
 
+    box_load = pltpu.make_async_copy(box_in, boxes_here, load_sems.at[4])
+    off_load = pltpu.make_async_copy(off_in, offs_here, load_sems.at[5])
     slots = lax.broadcasted_iota(jnp.int32, (NBR, NC), 0)
     rows_here[...] = jnp.where(slots < count_in[...], list_in[...] - (device * NC - NC), 3 * NC)
-    boxes_here[...] = box_in[...] * 8
-    offs_here[...] = off_in[...] * 8
     lists = []
     for k in range(NBR):
         lists.append(
             pltpu.make_async_copy(rows_here.at[k], where.at[pl.ds(k * NC, NC)], list_sems.at[k])
         )
-    for j in range(IL):
-        part = pl.ds(j * 4096, 4096)
-        lists.append(pltpu.make_async_copy(boxes_here.at[j], which_box.at[part], box_sems.at[j]))
-        lists.append(pltpu.make_async_copy(offs_here.at[j], which_off.at[part], off_sems.at[j]))
-    for copy in lists:
-        copy.start()
-
+        lists[-1].start()
     build_matrix(interp, angle, matrix, trig)
     piece[...] = jnp.zeros((32, 384), BF16)
     for c in range(2):
         piece[c * 16 : c * 16 + 16, 0:OFFS] = oper[c]
     loads[0].wait()
     loads[1].wait()
+    loads[2].start()
+    box_load.start()
+    off_load.start()
     leaf_patterns(window.at[1], rad, leaf)
     pack_leaves(leaf, packed)
     for at in range(16):
@@ -346,8 +346,8 @@
         to, to_device = moved(n, 1)
         return pltpu.make_async_remote_copy(
             src_ref=send.at[to],
-            dst_ref=rec.at[2 * chip + core],
-            send_sem=up_send.at[n],
+            dst_ref=rec.at[core, n],
+            send_sem=up_send,
             recv_sem=up_recv.at[n],
             device_id=to_device,
             device_id_type=MESH_ID,
@@ -357,11 +357,22 @@
         up_copy(n).start()
         return carry
 
-    lax.fori_loop(0, CHIPS - 1, up_start, 0)
+    lax.fori_loop(0, WINDOW, up_start, 0)
     own_piece = pltpu.make_async_copy(piece, pieces.at[z * 2 + core], load_sems.at[3])
     own_piece.start()
-    own = pltpu.make_async_copy(send.at[chip], rec.at[2 * chip + core], own_sem)
+    own = pltpu.make_async_copy(send.at[chip], rec.at[core, CHIPS - 1], own_sem)
     own.start()
+
+    box_load.wait()
+    off_load.wait()
+    boxes_here[...] = boxes_here[...] * 8
+    offs_here[...] = offs_here[...] * 8
+    for j in range(IL):
+        part = pl.ds(j * 4096, 4096)
+        lists.append(pltpu.make_async_copy(boxes_here.at[j], which_box.at[part], box_sems.at[j]))
+        lists[-1].start()
+        lists.append(pltpu.make_async_copy(offs_here.at[j], which_off.at[part], off_sems.at[j]))
+        lists[-1].start()
 
     own_piece.wait()
     for line in lines:
@@ -373,19 +384,18 @@
         shares[-1].start()
     own.wait()
 
-    def pass_copy(n):
-        at = rec.at[2 * moved(n, -1)[0] + core]
+    def pass_copy(m):
+        at = rec.at[core, pl.ds(m * GROUP, GROUP)]
         return pltpu.make_async_remote_copy(
             src_ref=at,
             dst_ref=at,
-            send_sem=pass_send.at[n],
-            recv_sem=pass_recv.at[n],
+            send_sem=pass_send,
+            recv_sem=pass_recv.at[m],
             device_id=sibling,
             device_id_type=MESH_ID,
         )
 
-    pass_copy(CHIPS - 1).start()
-    widen(rec, 2 * chip + core, field)
+    widen(rec, core, CHIPS - 1, 2 * chip + core, field)
     spread_currents(window, 1, ext)
     ext[3 * NC] = jnp.zeros((16, 128), BF16)
     to_sibling.wait()
@@ -402,46 +412,61 @@
             for k in range(4):
                 table[pl.ds(g * 1024 + c * 4 + k, 128, stride=8), :] = turned
     loads[2].wait()
-    for copy in lists:
+    for copy in lists[:NBR]:
         copy.wait()
 
     def arrive(n):
         up_copy(n).wait_recv()
-        pass_copy(n).start()
-        widen(rec, 2 * moved(n, -1)[0] + core, field)
-
-    def take(n):
-        source = moved(n, -1)[0]
-        at = rec.at[2 * source + 1 - core]
-        pltpu.make_async_copy(at, at, pass_recv.at[n]).wait()
-        widen(rec, 2 * source + 1 - core, field)
-
-    def near_step(b, carry):
-        near_box(b, blocks, where, ext, out)
-        arrive(2 * b)
-
-        @pl.when(b < 31)
+
+        @pl.when(n < CHIPS - 1 - WINDOW)
         def _():
-            arrive(2 * b + 1)
-
-        @pl.when(b >= 2)
+            up_copy(n + WINDOW).start()
+
+    def take(m):
+        at = rec.at[1 - core, pl.ds(m * GROUP, GROUP)]
+        pltpu.make_async_copy(at, at, pass_recv.at[m]).wait()
+        for k in range(GROUP):
+            n = m * GROUP + k
+            widen(rec, 1 - core, n, 2 * moved(n, -1)[0] + 1 - core, field)
+
+    def near_step(m, carry):
+        near_box(2 * m, blocks, where, ext, out)
+        near_box(2 * m + 1, blocks, where, ext, out)
+        for k in range(GROUP - 1):
+            arrive(m * GROUP + k)
+
+        @pl.when(m < CHIPS // GROUP - 1)
         def _():
-            take(2 * b - 4)
-            take(2 * b - 3)
-
-        return carry
-
-    lax.fori_loop(0, BOXES, near_step, 0)
-    for n in range(CHIPS - 4, CHIPS):
-        take(n)
+            arrive(m * GROUP + GROUP - 1)
+
+        pass_copy(m).start()
+        for k in range(GROUP - 1):
+            n = m * GROUP + k
+            widen(rec, core, n, 2 * moved(n, -1)[0] + core, field)
+
+        @pl.when(m < CHIPS // GROUP - 1)
+        def _():
+            n = m * GROUP + GROUP - 1
+            widen(rec, core, n, 2 * moved(n, -1)[0] + core, field)
+
+        @pl.when(m >= 1)
+        def _():
+            take(m - 1)
+
+        return carry
+
+    lax.fori_loop(0, CHIPS // GROUP, near_step, 0)
+    take(CHIPS // GROUP - 1)
+    for copy in lists[NBR:]:
+        copy.wait()
 
     def down_copy(n):
         to, to_device = moved(n, 1)
         return pltpu.make_async_remote_copy(
             src_ref=send2.at[to],
             dst_ref=rec2.at[chip],
-            send_sem=down_send.at[n],
-            recv_sem=down_recv.at[n],
+            send_sem=down_send,
+            recv_sem=down_recv,
             device_id=to_device,
             device_id_type=MESH_ID,
         )
@@ -461,20 +486,15 @@
     last = pltpu.make_async_copy(send2.at[chip], rec2.at[chip], own_sem)
     last.start()
 
-    def up_done(n, carry):
-        up_copy(n).wait_send()
-        pass_copy(n).wait_send()
-        return carry
-
-    lax.fori_loop(0, CHIPS - 1, up_done, 0)
-    pass_copy(CHIPS - 1).wait_send()
+    def settle(ref, sem):
+        pltpu.make_async_copy(ref, ref, sem).wait()
+
+    settle(send.at[pl.ds(0, CHIPS - 1)], up_send)
+    settle(rec.at[core], pass_send)
     last.wait()
 
-    def down_done(n, carry):
-        down_copy(n).wait()
-        return carry
-
-    lax.fori_loop(0, CHIPS - 1, down_done, 0)
+    settle(send2.at[pl.ds(0, CHIPS - 1)], down_send)
+    settle(rec2.at[pl.ds(0, CHIPS - 1)], down_recv)
     unpack_fields(rec2, matrix, leaf)
     far_boxes(leaf, rad, out)
 
@@ -485,7 +505,7 @@
     return pl.pallas_call(
         main_kernel,
         out_shape=jax.ShapeDtypeStruct((16, NC * U), F32),
-        in_specs=[any_spec] * 3 + [VMEM_SPEC] * 7,
+        in_specs=[any_spec] * 3 + [VMEM_SPEC] * 5 + [any_spec] * 2,
         out_specs=VMEM_SPEC,
         scratch_shapes=[
             pltpu.VMEM((1024, 2048), BF16),
@@ -497,7 +517,7 @@
             pltpu.VMEM((3, 16, NC * U), BF16),
             pltpu.VMEM((3 * NC + 1, 16, 128), BF16),
             pltpu.VMEM((CHIPS, 2, 2, BOXES, 128), BF16),
-            pltpu.VMEM((2 * CHIPS, 2, 2, BOXES, 128), BF16),
+            pltpu.VMEM((2, CHIPS, 2, 2, BOXES, 128), BF16),
             pltpu.VMEM((32, 384), BF16),
             pltpu.VMEM((8, 32, 384), BF16),
             pltpu.VMEM((4096 * 8, 128), F32),
@@ -511,16 +531,16 @@
             pltpu.SMEM((NC * NBR,), jnp.int32),
             pltpu.SMEM((4096 * IL,), jnp.int32),
             pltpu.SMEM((4096 * IL,), jnp.int32),
-            sems((4,)),
+            sems((6,)),
             sems((NBR,)),
             sems((IL,)),
             sems((IL,)),
+            sems,
             sems((CHIPS,)),
-            sems((CHIPS,)),
-            sems((CHIPS,)),
-            sems((CHIPS,)),
-            sems((CHIPS,)),
-            sems((CHIPS,)),
+            sems,
+            sems((CHIPS // GROUP,)),
+            sems,
+            sems,
             sems((9,)),
             sems((9,)),
             sems,

time: 114 us -> 105 us (0.921); the launches traced: 114 us -> 103 us
  Pallas kernels: 112 us -> 101 us
    pallas_call x1, Pallas kernels: 112 us -> 101 us  [main_part(): pl.pallas_call(main_kernel, out_shape=jax.ShapeDtypeStruct((16, NC * U),...]
where the time goes in v4:
time: 105 us; the launch traced here: 103 us
  Pallas kernels  101 us (96%)
  local copies, waits for them, and re-layouts  1.87 us (2%)
    pallas_call x1, Pallas kernels, main_part(): pl.pallas_call(main_kernel, out_shape=jax.ShapeDtypeStruct((16, NC * U),...  101 us

profile of v4, /device:TPU:1, one launch (start us, length us, event | category | flops | bytes accessed | tf_op | source)
XLA Modules:
  0.0 103.3 jit_solution(16888366982029697857)
XLA Ops:
  0.0 101.5 %up_near_translate.1 = f32[16,8192]{1,0:T(8,128)} custom-call(bf16[16,8192]{1,0:T(8,128)(2,1)} %bitcast.8, bf16[2,256,32,256]{3,2,1,0:T(8,128)(2,1)} %blocks_in.1, bf16[2,256,32,128]{3,2,1,0:T(8,128)(2,1)} %rad_in.1, bf16[64,1024]{1,0:T(8,128)(2,1)} %interp.1, f32[8,1024]{1,0:T(8,128)} %angle.1, bf16[2,16,316]{2,1,0:T(8,128)(2,1)} %bitcast.11, ...), custom_call_target="tpu_custom_call" | custom-call | tf_op jit(solution)/shard_map/up_near_translate/pallas_call | solution.py:505
  101.5 1.9 %copy.12 = f32[2,8,8192]{2,1,0:T(8,128)} copy(f32[2,8,8192]{2,1,0:T(8,128)} %bitcast.7) | data formatting | bytes 1048576

commit v5 on v4

--- a/solution.py
+++ b/solution.py
@@ -81,7 +81,7 @@
             leaf[pl.ds((8 + i) * 256 + b, 8, stride=32), :] = by_imag[lo] + by_real[hi]
         return carry
 
-    lax.fori_loop(0, BOXES, box, 0, unroll=2)
+    lax.fori_loop(0, BOXES, box, 0, unroll=8)
 
 
 def pack_leaves(leaf, packed):
@@ -149,7 +149,7 @@
         field[pl.ds(device * 256 + k + 4, 32, stride=8), :] = value
 
 
-def translate_chunk(base, which_box, which_off, field, table, sums, out, chip):
+def translate_chunk(base, which_box, which_off, field, table, sums):
     starts = [base + j * 4096 for j in range(IL)]
     for b in range(BOXES):
         total = None
@@ -159,6 +159,9 @@
             term = field[pl.ds(row, 8), :] * table[pl.ds(operator, 8), :]
             total = term if total is None else total + term
         sums[b * 8 : b * 8 + 8, :] = total
+
+
+def combine_chunk(sums, out, chip):
     parts = [sums[pl.ds(k, BOXES, stride=8), :] for k in range(8)]
     out[chip, 0, 0] = (parts[0] - parts[5]).astype(BF16)
     out[chip, 0, 1] = (parts[1] + parts[4]).astype(BF16)
@@ -210,7 +213,7 @@
         out[8:16, lanes] += real[8:16] - imag[0:8]
         return carry
 
-    lax.fori_loop(0, BOXES, box, 0, unroll=2)
+    lax.fori_loop(0, BOXES, box, 0, unroll=8)
 
 
 def main_kernel(
@@ -472,17 +475,19 @@
         )
 
     def chunk(n, carry):
-        to = moved(n, 1)[0]
-        base = to * 64 + core * 32
-        translate_chunk(base, which_box, which_off, field, table, sums, send2, to)
-
-        @pl.when(n < CHIPS - 1)
+        combine_chunk(sums, send2, moved(n - 1, 1)[0])
+        base = moved(n, 1)[0] * 64 + core * 32
+        translate_chunk(base, which_box, which_off, field, table, sums)
+
+        @pl.when(n >= 1)
         def _():
-            down_copy(n).start()
+            down_copy(n - 1).start()
 
         return carry
 
+    sums[...] = jnp.zeros((BOXES * 8, 128), F32)
     lax.fori_loop(0, CHIPS, chunk, 0)
+    combine_chunk(sums, send2, chip)
     last = pltpu.make_async_copy(send2.at[chip], rec2.at[chip], own_sem)
     last.start()
 

time: 105 us -> 102 us (0.971)
  Pallas kernels: 101 us -> 99.3 us
    pallas_call x1, Pallas kernels: 101 us -> 99.3 us  [main_part(): pl.pallas_call(main_kernel, out_shape=jax.ShapeDtypeStruct((16, NC * U),...]
where the time goes in v5:
time: 102 us; the launch traced here: 101 us
  Pallas kernels  99.3 us (97%)
  local copies, waits for them, and re-layouts  1.87 us (2%)
    pallas_call x1, Pallas kernels, main_part(): pl.pallas_call(main_kernel, out_shape=jax.ShapeDtypeStruct((16, NC * U),...  99.3 us

profile of v5, /device:TPU:1, one launch (start us, length us, event | category | flops | bytes accessed | tf_op | source)
XLA Modules:
  0.0 101.2 jit_solution(11051900320172692969)
XLA Ops:
  0.0 99.3 %up_near_translate.1 = f32[16,8192]{1,0:T(8,128)} custom-call(bf16[16,8192]{1,0:T(8,128)(2,1)} %bitcast.8, bf16[2,256,32,256]{3,2,1,0:T(8,128)(2,1)} %blocks_in.1, bf16[2,256,32,128]{3,2,1,0:T(8,128)(2,1)} %rad_in.1, bf16[64,1024]{1,0:T(8,128)(2,1)} %interp.1, f32[8,1024]{1,0:T(8,128)} %angle.1, bf16[2,16,316]{2,1,0:T(8,128)(2,1)} %bitcast.11, ...), custom_call_target="tpu_custom_call" | custom-call | tf_op jit(solution)/shard_map/up_near_translate/pallas_call | solution.py:510
  99.3 1.9 %copy.12 = f32[2,8,8192]{2,1,0:T(8,128)} copy(f32[2,8,8192]{2,1,0:T(8,128)} %bitcast.7) | data formatting | bytes 1048576

commit v6 on v5

--- a/solution.py
+++ b/solution.py
@@ -174,15 +174,16 @@
     for c in range(2):
         for half in range(2):
             rows = slice(c * 512 + half * 256, c * 512 + half * 256 + 256)
-            results = []
+            both = []
             for p in range(2):
                 pieces = []
                 for block in range(8):
                     for c2 in range(2):
                         at = (p * 8 + block) * 4
                         pieces.append(rec2[at : at + 4, :, c2].reshape(256, 128))
-                fields = jnp.concatenate(pieces, axis=1)
-                results.append(dot_t(fields, matrix[rows, :]))
+                both.append(jnp.concatenate(pieces, axis=1))
+            result = dot_t(jnp.concatenate(both, axis=0), matrix[rows, :])
+            results = [result[0:256], result[256:512]]
             for m in range(2):
                 first = results[0][:, m * 128 : m * 128 + 128]
                 second = results[1][:, m * 128 : m * 128 + 128]
@@ -316,12 +317,15 @@
     off_load.start()
     leaf_patterns(window.at[1], rad, leaf)
     pack_leaves(leaf, packed)
-    for at in range(16):
-        lanes = slice(at % 8 * 256, at % 8 * 256 + 256)
-        result = dot(packed[at // 8], matrix[:, lanes]).astype(BF16)
-        for r in range(R):
-            for c in range(2):
-                send[at * 4 + r // 2, r % 2, c] = result[r * 32 : r * 32 + 32, c * 128 : c * 128 + 128]
+    for block in range(8):
+        lanes = slice(block * 256, block * 256 + 256)
+        result = dot(packed[...].reshape(512, 1024), matrix[:, lanes]).astype(BF16)
+        for p in range(2):
+            for r in range(R):
+                rows = slice(p * 256 + r * 32, p * 256 + r * 32 + 32)
+                for c in range(2):
+                    at = (p * 8 + block) * 4 + r // 2
+                    send[at, r % 2, c] = result[rows, c * 128 : c * 128 + 128]
 
     pl.semaphore_wait(barrier, CHIPS + 1)
 

time: 102 us -> 102 us (level)
  no operation moved by 1% of the time
where the time goes in v6:
time: 102 us; the launch traced here: 101 us
  Pallas kernels  99.4 us (97%)
  local copies, waits for them, and re-layouts  1.87 us (2%)
    pallas_call x1, Pallas kernels, main_part(): pl.pallas_call(main_kernel, out_shape=jax.ShapeDtypeStruct((16, NC * U),...  99.4 us

profile of v6, /device:TPU:1, one launch (start us, length us, event | category | flops | bytes accessed | tf_op | source)
XLA Modules:
  0.0 101.3 jit_solution(6982927137211519388)
XLA Ops:
  0.0 99.4 %up_near_translate.1 = f32[16,8192]{1,0:T(8,128)} custom-call(bf16[16,8192]{1,0:T(8,128)(2,1)} %bitcast.8, bf16[2,256,32,256]{3,2,1,0:T(8,128)(2,1)} %blocks_in.1, bf16[2,256,32,128]{3,2,1,0:T(8,128)(2,1)} %rad_in.1, bf16[64,1024]{1,0:T(8,128)(2,1)} %interp.1, f32[8,1024]{1,0:T(8,128)} %angle.1, bf16[2,16,316]{2,1,0:T(8,128)(2,1)} %bitcast.11, ...), custom_call_target="tpu_custom_call" | custom-call | tf_op jit(solution)/shard_map/up_near_translate/pallas_call | solution.py:514
  99.4 1.9 %copy.12 = f32[2,8,8192]{2,1,0:T(8,128)} copy(f32[2,8,8192]{2,1,0:T(8,128)} %bitcast.7) | data formatting | bytes 1048576
